TPU v7x, 128 devices: a whole 4x4x4 slice. The times are simulated.
128 devices in a mesh: row: 8 (over x_lo, y), col: 16 (over x_hi, z, core).
Axes of the slice: x: 4 (x_hi: 2, x_lo: 2; x = x_hi * 2 + x_lo), y: 4, z: 4, core: 2. Of those that a mesh axis runs over, the one named last changes fastest.
Arguments:
- positions: float32 [3, 393216], P(None, ('row', 'col')), may hold values from -1 to 1
- normals: float32 [3, 393216], P(None, ('row', 'col')), may hold values from -4 to 4
- patch_extents: float32 [393216], P(('row', 'col')), may hold values from 0.02 to 0.2
- mirrored_fraction: float32 [393216], P(('row', 'col')), may hold values from 0.1 to 0.9
- inner_emission_power: float32 [393216], P(('row', 'col')), may hold values from 0.1 to 1
- radiosity: float32 [393216], P(('row', 'col')), may hold values from 0.2 to 2
- basis: float32 [8, 393216], P(None, ('row', 'col')), may hold values from -6 to 6
- recv_blocks: int32 [8, 16, 512], P('row', 'col'), may hold values from 0 to 191
- emit_blocks: int32 [8, 16, 512], P('row', 'col'), may hold values from 0 to 383
- vis_count: int32 [8, 16], P('row', 'col'), may hold values from 128 to 512, as said below
- owner: int32 [393216, 1], P(('row', 'col')), may hold values from 0 to 127; in each aligned block of 3072 rows (0 to 3071, 3072 to 6143, ...) at most 96 rows name the same one
- local_elem: int32 [393216], P(('row', 'col')), may hold values from 0 to 2047
Outputs:
- new_vector: float32 [393216], P(('row', 'col'))
- hessen: float32 [9], replicated
- element_loads: float32 [262144], P(('row', 'col'))
Inputs may be any that keep to these rules, and one draw needn't show every extreme that they name: `vis_count`: some device has 512 live entries in every draw. Among the patches of one device no owner is named more than 96 times; that many is reached.
All inputs are finite; a program needn't handle non-finite values.
Results may differ from a plain program's by a relative error of at most 0.0003.
Values sent between devices are 32-bit elements; how exact they have to be, the bound alone decides.
No kernel may reach another device: no remote copies, remote signals or barrier semaphores. Data moves between devices by JAX's collectives and lax.ppermute only.
A program may use at most 64 MiB of HBM per device.

v0:
```python
import jax
import jax.numpy as jnp
from jax import lax
from jax.sharding import PartitionSpec as P

E_DEV = 2048


def view_terms(receiver, emitter, vectors):
    offset = emitter[0:3, :, None, :] - receiver[0:3, :, :, None]
    facing = jnp.maximum(jnp.sum(receiver[3:6, :, :, None] * offset, axis=0), 0.0)
    destination_index = jnp.maximum(-jnp.sum(emitter[3:6, :, None, :] * offset, axis=0), 0.0)
    area_row = emitter[6][:, None, :]
    spread = jnp.sum(offset * offset, axis=0) + area_row
    factor = facing * destination_index * area_row / (jnp.pi * spread * spread)
    return jnp.einsum("gre,kge->kgr", factor, vectors, precision=lax.Precision.HIGHEST)


def group_sum(totals, recv_tiles, emit_tiles, receiver_selection, emit_pick, weight_pick):
    recv_part = jnp.take(recv_tiles, receiver_selection, axis=1)
    emit_part = jnp.take(emit_tiles, emit_pick, axis=1)
    contrib = view_terms(recv_part, emit_part[0:7], emit_part[7:9]) * weight_pick[None, :, None]
    return totals.at[:, receiver_selection].add(contrib)


def window_of(array, round_at):
    return lax.dynamic_slice_in_dim(array, round_at * 16, 16)


def shards(
    positions,
    normals,
    patch_extents,
    mirrored_fraction,
    inner_emission_power,
    radiosity,
    basis,
    recv_blocks,
    emit_blocks,
    vis_count,
    owner,
    local_elem,
):
    patches = positions.shape[1]
    tiles_dev = patches // 128
    krylov = basis[-1]
    receiver = jnp.concatenate([positions, normals], axis=0).reshape(6, tiles_dev, 128)
    recv_tiles = lax.all_gather(receiver, "row", axis=1, tiled=True)
    emitter = jnp.concatenate(
        [positions, normals, patch_extents[None], radiosity[None], krylov[None]], axis=0
    ).reshape(9, tiles_dev, 128)
    recv_list = recv_blocks.reshape(-1)
    emit_list = emit_blocks.reshape(-1)
    listed = recv_list.shape[0]
    live_mask = (jnp.arange(listed, dtype=jnp.int32) < vis_count.reshape(())).astype(jnp.float32)
    totals = jnp.zeros((2, recv_tiles.shape[1], 128), jnp.float32)
    rounds = listed // 16
    emit_tiles = lax.all_gather(emitter, "col", axis=1, tiled=True)

    def advance(round_at, carried):
        return group_sum(
            carried,
            recv_tiles,
            emit_tiles,
            window_of(recv_list, round_at),
            window_of(emit_list, round_at),
            window_of(live_mask, round_at),
        )

    totals = lax.fori_loop(0, rounds, advance, totals)
    summed = lax.psum(totals, "row")
    own_rows = lax.dynamic_slice_in_dim(summed, lax.axis_index("row") * tiles_dev, tiles_dev, 1)
    own_rows = own_rows.reshape(2, patches)
    arriving_power_density = own_rows[0]
    scattered = own_rows[1]
    applied = krylov - mirrored_fraction * scattered
    cell_count = patches * lax.axis_size("row") * lax.axis_size("col")
    projection_weights = (
        lax.psum(jnp.dot(basis, applied, precision=lax.Precision.HIGHEST), ("row", "col"))
        / cell_count
    )
    leftover_residual = applied - jnp.dot(
        projection_weights, basis, precision=lax.Precision.HIGHEST
    )
    length = jnp.sqrt(
        lax.psum(jnp.sum(leftover_residual * leftover_residual), ("row", "col")) / cell_count
        + 1e-06
    )
    new_vector = leftover_residual / length
    hessen = jnp.concatenate([projection_weights, length[None]])
    plate_kelvin_level = (
        (1.0 - mirrored_fraction) * arriving_power_density + inner_emission_power
    ) ** 0.25
    boundary_warming_demand = 20.0 * patch_extents * plate_kelvin_level
    devices = lax.axis_size("row") * lax.axis_size("col")
    capacity = 4 * patches // devices
    target = owner[:, 0]
    onehot = (target[:, None] == jnp.arange(devices, dtype=jnp.int32)[None, :]).astype(jnp.int32)
    before = jnp.cumsum(onehot, axis=0) - onehot
    slot_position = jnp.sum(before * onehot, axis=1)
    slot_index = target * capacity + slot_position
    values = (
        jnp.zeros((devices * capacity,), jnp.float32).at[slot_index].set(boundary_warming_demand)
    )
    element = jnp.zeros((devices * capacity,), jnp.int32).at[slot_index].set(local_elem)
    arrived, target_slots = (
        lax.all_to_all(
            values.reshape(devices, capacity),
            ("row", "col"),
            split_axis=0,
            concat_axis=0,
            tiled=True,
        ),
        lax.all_to_all(
            element.reshape(devices, capacity),
            ("row", "col"),
            split_axis=0,
            concat_axis=0,
            tiled=True,
        ),
    )
    element_loads = (
        jnp.zeros((E_DEV,), jnp.float32).at[target_slots.reshape(-1)].add(arrived.reshape(-1))
    )
    return (new_vector, hessen, element_loads)


def solution(mesh):
    in_specs = (
        P(None, ("row", "col")),
        P(None, ("row", "col")),
        P(("row", "col")),
        P(("row", "col")),
        P(("row", "col")),
        P(("row", "col")),
        P(None, ("row", "col")),
        P("row", "col", None),
        P("row", "col", None),
        P("row", "col"),
        P(("row", "col"), None),
        P(("row", "col")),
    )
    out_specs = (P(("row", "col")), P(), P(("row", "col")))
    return jax.shard_map(shards, mesh=mesh, in_specs=in_specs, out_specs=out_specs, check_vma=False)
```

profile of v0, /device:TPU:1, one launch (start us, length us, event | category | flops | bytes accessed | tf_op | source)
XLA Modules:
  0.0 678.7 jit_solution(12235389546444212587)
XLA Ops:
  12.8 24.8 %all_gather.7 = f32[6,192,128]{2,1,0:T(8,128)S(1)} all-gather(f32[6,24,128]{2,1,0:T(8,128)S(1)} %bitcast.62), channel_id=1, replica_groups=mesh['row'=8,'col'=16] {'row'}, dimensions={1}, use_global_device_ids=true | all-gather | bytes 663552 | tf_op jit(solution)/shard_map/all_gather | solution.py:48
  41.0 2.4 fusion.12
  43.5 19.4 %all-gather.2.cloned.1.call-done = f32[9,384,128]{2,1,0:T(8,128)} async-done(((f32[9,24,128]{2,1,0:T(8,128)}), f32[9,384,128]{2,1,0:T(8,128)}) %all-gather.2.cloned.1.call-update) | async-done | bytes 1769488 | tf_op jit(solution)/shard_map/all_gather | solution.py:58
  62.8 2.6 copy.38
  65.5 298.5 %while.13 = (s32[]{:T(128)}, f32[2,192,128]{2,0,1:T(2,128)S(1)}, s32[512]{0:T(512)}, s32[512]{0:T(512)}, f32[9,384,128]{2,0,1:T(8,128)S(1)}, /*index=5*/f32[6,19...) while((s32[]{:T(128)}, f32[2,192,128]{2,0,1:T(2,128)S(1)}, ...), condition=%wide.region_5.6_spmd, body=%wide.region_0.5_spmd.sunk | while | flops 13410502 | bytes 7390635 | solution.py:70
  68.9 2.2 fusion.39
  71.8 1.9 convolution_multiply_fusion.2
  78.2 2.2 fusion.39
  81.1 1.9 convolution_multiply_fusion.2
  87.5 2.2 fusion.39
  90.5 1.9 convolution_multiply_fusion.2
  96.8 2.2 fusion.39
  99.8 1.9 convolution_multiply_fusion.2
  106.2 2.2 fusion.39
  109.1 1.9 convolution_multiply_fusion.2
  115.5 2.2 fusion.39
  118.4 1.9 convolution_multiply_fusion.2
  124.8 2.2 fusion.39
  127.8 1.9 convolution_multiply_fusion.2
  134.2 2.2 fusion.39
  137.1 1.9 convolution_multiply_fusion.2
  143.5 2.2 fusion.39
  146.4 1.9 convolution_multiply_fusion.2
  152.8 2.2 fusion.39
  155.8 1.9 convolution_multiply_fusion.2
  162.1 2.2 fusion.39
  165.1 1.9 convolution_multiply_fusion.2
  171.5 2.2 fusion.39
  174.4 1.9 convolution_multiply_fusion.2
  180.8 2.2 fusion.39
  183.7 1.9 convolution_multiply_fusion.2
  190.1 2.2 fusion.39
  193.1 1.9 convolution_multiply_fusion.2
  199.5 2.2 fusion.39
  202.4 1.9 convolution_multiply_fusion.2
  208.8 2.2 fusion.39
  211.7 1.9 convolution_multiply_fusion.2
  218.1 2.2 fusion.39
  221.1 1.9 convolution_multiply_fusion.2
  227.4 2.2 fusion.39
  236.8 2.2 fusion.39
  246.1 2.2 fusion.39
  255.4 2.2 fusion.39
  264.8 2.2 fusion.39
  274.1 2.2 fusion.39
  283.4 2.2 fusion.39
  292.8 2.2 fusion.39
  302.1 2.2 fusion.39
  311.4 2.2 fusion.39
  320.7 2.2 fusion.39
  330.1 2.2 fusion.39
  339.4 2.2 fusion.39
  348.7 2.2 fusion.39
  358.1 2.2 fusion.39
  365.5 12.0 %scatter_custom_fusion.1 = s32[12288]{0:T(1024)S(1)} fusion(s32[3072]{0:T(1024)S(1)} %bitcast.76, s32[3072]{0:T(1024)} %param.25, s32[]{:T(128)} %constant.122.clone.1), kind=kCustom, calls=%fused_computation.47 | custom fusion | bytes 49664 | tf_op jit(solution)/shard_map/scatter | solution.py:105
  378.1 6.6 all-to-all-start
  384.8 9.6 %all-to-all-done = s32[128,1,96]{2,1,0:T(1,128)S(1)} async-done(((s32[128,1,96]{2,1,0:T(1,128)}), s32[128,1,96]{2,1,0:T(1,128)S(1)}, u32[]{:S(2)}, u32[]{:S(2)}) %all-to-all-start) | async-done | bytes 49184 | tf_op jit(solution)/shard_map/all_to_all | solution.py:114
  395.9 36.1 %all-reduce.2.cloned.1.call-done = f32[2,192,128]{2,0,1:T(2,128)} async-done(((f32[2,192,128]{2,0,1:T(2,128)}), f32[2,192,128]{2,0,1:T(2,128)}) %all-reduce.2.cloned.1.call-update) | async-done | bytes 196624 | tf_op jit(solution)/shard_map/psum | solution.py:71
  434.9 69.1 %psum.22 = f32[8]{0:T(128)S(1)} all-reduce(f32[8]{0:T(128)S(1)} %convolution_bitcast_fusion), channel_id=1, replica_groups=mesh['row'=8,'col'=16] {'row','col'}, use_global_device_ids=true, to_apply=%region_7.8 | all-reduce | flops 8 | bytes 64 | tf_op jit(solution)/shard_map/psum | solution.py:79
  505.7 62.7 %psum.23 = f32[]{:T(128)} all-reduce(f32[]{:T(128)} %get-tuple-element.163), channel_id=1, replica_groups=mesh['row'=8,'col'=16] {'row','col'}, use_global_device_ids=true, to_apply=%region_9.10 | all-reduce | flops 1 | bytes 8 | tf_op jit(solution)/shard_map/psum | solution.py:86
  569.2 11.8 %scatter_custom_fusion.2 = f32[12288]{0:T(1024)S(1)} fusion(s32[3072]{0:T(1024)S(1)} %bitcast.77, f32[3072]{0:T(1024)S(1)} %get-tuple-element.173, f32[]{:T(128)} %constant.123.clone.1), kind=kCustom, calls=%fused_computation.45 | custom fusion | bytes 49156 | tf_op jit(solution)/shard_map/scatter | solution.py:103
  581.7 5.4 all-to-all-start.1
  588.2 8.4 %all-to-all-done.1 = f32[128,1,96]{2,1,0:T(1,128)S(1)} async-done(((f32[128,1,96]{2,1,0:T(1,128)}), f32[128,1,96]{2,1,0:T(1,128)S(1)}, u32[]{:S(2)}, u32[]{:S(2)}) %all-to-all-start.1) | async-done | bytes 49184 | tf_op jit(solution)/shard_map/all_to_all | solution.py:107
  598.1 73.8 %scatter_custom_fusion.3 = f32[2048]{0:T(1024)} fusion(s32[12288]{0:T(1024)S(1)} %bitcast.72, f32[12288]{0:T(1024)S(1)} %reshape.159, f32[]{:T(128)} %constant.123.clone.1), kind=kCustom, calls=%fused_computation.57 | custom fusion | flops 12288 | bytes 8196 | tf_op jit(solution)/shard_map/scatter-add | solution.py:123
  (575 shorter events, 212.7 us)
Async XLA Ops:
  7.2 32.2 %copy-start.2 = (s32[3072,1]{0,1:T(1,128)S(1)}, s32[3072,1]{0,1:T(1,128)}, u32[]{:S(2)}) copy-start(s32[3072,1]{0,1:T(1,128)} %param.24) | copy-start | bytes 36868
  7.2 55.7 %all-gather.2.cloned.1.call-start = ((), (), s32[]{:S(2)}) async-start(), calls=%async_computation.2 | async-start | bytes 1880064 | tf_op jit(solution)/shard_map/all_gather | solution.py:58
  8.9 2.2 copy-start.3
  11.2 0.6 copy-start.1
  11.8 420.1 %all-reduce.2.cloned.1.call-start = ((), (), s32[]{:S(2)}) async-start(), calls=%async_computation.3 | async-start | bytes 393216 | tf_op jit(solution)/shard_map/psum | solution.py:71
  364.0 0.7 copy-start
  378.1 16.3 %all-to-all-start = ((s32[128,1,96]{2,1,0:T(1,128)}), s32[128,1,96]{2,1,0:T(1,128)S(1)}, u32[]{:S(2)}, u32[]{:S(2)}) async-start(s32[128,1,96]{2,1,0:T(1,128)} %bitcast.23), calls=%async_computation | async-start | bytes 131072 | tf_op jit(solution)/shard_map/all_to_all | solution.py:114
  581.7 15.0 %all-to-all-start.1 = ((f32[128,1,96]{2,1,0:T(1,128)}), f32[128,1,96]{2,1,0:T(1,128)S(1)}, u32[]{:S(2)}, u32[]{:S(2)}) async-start(f32[128,1,96]{2,1,0:T(1,128)} %bitcast.26), calls=%async_computation.1 | async-start | bytes 131072 | tf_op jit(solution)/shard_map/all_to_all | solution.py:107
Sparse Core Ops, SparseCore 0:
  12.0 50.8 all-gather.1
  364.8 67.0 all-reduce.1
where the time goes:
time: 689 us; the launch traced here: 679 us
  other arithmetic  218 us (32%)
  blocking collectives  157 us (23%)
  local copies, waits for them, and re-layouts  135 us (20%)
  waiting for transfers between devices  73.5 us (11%)
  matrix products  63.1 us (9%)
  between operations  15.6 us (2%)
  starting transfers between devices  12.1 us (2%)
    scatter-add x1, other arithmetic, shards(): jnp.zeros((E_DEV,), jnp.float32).at[target_slots.reshape(-1)]  73.8 us
    psum x1, blocking collectives, shards(): lax.psum(jnp.dot(basis, applied, precision=lax.Precision.HIGHEST), ('row'...  69.1 us
    reduce_sum x32, other arithmetic, view_terms(): jnp.sum(receiver[3:6, :, :, None] * offset, axis=0)  69.1 us
    psum x1, blocking collectives, shards(): lax.psum(jnp.sum(leftover_residual * leftover_residual), ('row', 'col'))  62.7 us
    dot_general x32, matrix products, view_terms(): jnp.einsum('gre,kge->kgr', factor, vectors, precision=lax.Precision.HIGHEST)  60.8 us
    gather x32, local copies, waits for them, and re-layouts, group_sum(): recv_part = jnp.take(recv_tiles, receiver_selection, axis=1)  54.1 us
    psum x1, waiting for transfers between devices, shards(): summed = lax.psum(totals, 'row')  36.1 us
    scatter-add x32, other arithmetic, group_sum(): return totals.at[:, receiver_selection].add(contrib)  35.4 us
  transfers between devices with their start and end apart: 4, of which 4 were waited for; matrix products, arithmetic and copies ran while one was open for 3% of the time, Pallas kernels for 0%

commit v1 on v0

v1 whole, which is shorter than its diff:
```python
import functools
import math

import jax
import jax.numpy as jnp
from jax import lax
from jax.experimental import pallas as pl
from jax.experimental.pallas import tpu as pltpu
from jax.sharding import PartitionSpec as P

F32 = jnp.float32
BF16 = jnp.bfloat16
LANES = 128
E_DEV = 2048
NT = (((1,), (1,)), ((), ()))
TN = (((0,), (0,)), ((), ()))
VMEM = pl.BlockSpec(memory_space=pltpu.VMEM)
SMEM = pl.BlockSpec(memory_space=pltpu.SMEM)
LIMIT = 48 * 2**20


def split3(value):
    high = value.astype(BF16).astype(F32)
    rest = value - high
    middle = rest.astype(BF16).astype(F32)
    return high, middle, rest - middle


def call(body, out_shape, scratch=(), in_specs=None, name=None, cost=None):
    return pl.pallas_call(
        body,
        out_shape=out_shape,
        in_specs=in_specs,
        out_specs=jax.tree.map(lambda _: VMEM, out_shape),
        scratch_shapes=list(scratch),
        compiler_params=pltpu.CompilerParams(vmem_limit_bytes=LIMIT),
        cost_estimate=cost,
        name=name,
    )


def stage_kernel(tiles, n_col, n_row, pos, nor, area, rad, kry, emit, recv):
    x = [pos[k * tiles : (k + 1) * tiles] for k in range(3)]
    n = [nor[k * tiles : (k + 1) * tiles] for k in range(3)]
    a = area[...]
    b = rad[...]
    weight = a * b * (1.0 / math.pi)
    m = [weight * v for v in n]
    square = x[0] * x[0] + x[1] * x[1] + x[2] * x[2]
    emit_rows = x + m + [-(m[0] * x[0] + m[1] * x[1] + m[2] * x[2]), square + a]
    recv_rows = x + n + [-(n[0] * x[0] + n[1] * x[1] + n[2] * x[2]), square]
    ratio = kry[...] / b
    for c in range(n_col):
        base = c * 9 * tiles
        for f in range(8):
            emit[pl.ds(base + f, tiles, stride=8), :] = emit_rows[f]
        emit[base + 8 * tiles : base + 9 * tiles, :] = ratio
    for r in range(n_row):
        for f in range(8):
            recv[pl.ds(r * 8 * tiles + f, tiles, stride=8), :] = recv_rows[f]


def rank_kernel(tiles, owner, elem, basis, rank, slots, gram):
    sub = lax.broadcasted_iota(jnp.int32, (LANES, LANES), 0)
    lane = lax.broadcasted_iota(jnp.int32, (LANES, LANES), 1)
    upper = jnp.concatenate([(sub < lane).astype(BF16), jnp.ones((LANES, LANES), BF16)], 1)
    carry = jnp.zeros((LANES, LANES), F32)
    found = jnp.zeros((LANES, 2 * LANES), F32)
    for g in range(tiles):
        named = owner[g : g + 1, :] == sub
        hot = jnp.where(named, 1.0, 0.0)
        counts = jnp.dot(hot.astype(BF16), upper, preferred_element_type=F32)
        place = jnp.sum(hot * (counts[:, :LANES] + carry), axis=0, keepdims=True)
        carry = carry + counts[:, LANES:]
        place = place.astype(jnp.int32)
        rank[g : g + 1, :] = place
        index = elem[g : g + 1, :]
        high = (index >> 7).astype(F32)
        low = (index & 127).astype(F32)
        at = place == sub
        table = jnp.concatenate([jnp.where(at, high, 0.0), jnp.where(at, low, 0.0)], 0)
        found = found + lax.dot_general(
            hot.astype(BF16), table.astype(BF16), NT, preferred_element_type=F32
        )
    slots[...] = found[:, :LANES] * 128.0 + found[:, LANES:]
    lanes = lax.broadcasted_iota(jnp.int32, (1, LANES), 1)
    total = jnp.zeros((1, LANES), F32)
    at = 0
    for i in range(8):
        for j in range(i, 8):
            value = jnp.sum(
                basis[i * tiles : (i + 1) * tiles] * basis[j * tiles : (j + 1) * tiles],
                axis=(0, 1),
                keepdims=True,
            )
            total = total + jnp.where(lanes == at, value, 0.0)
            at += 1
    gram[...] = total


def pair_kernel(tiles, n_row, n_col, unroll, count, recv_list, emit_list, emit, recv, out, etab, wtab, wone, acc):
    row = lax.broadcasted_iota(jnp.int32, (8, LANES), 0)
    zero = jnp.zeros((8, LANES), F32)
    ones3 = jnp.where(row < 3, 1.0, 0.0)

    def recv_body(r, _):
        block = recv[pl.ds(pl.multiple_of(r * 8, 8), 8), :]
        parts = split3(block)
        facing, away, spread = [], [], []
        for k, part in enumerate(parts):
            one = 1.0 if k == 0 else 0.0
            facing.append(jnp.where(row < 3, pltpu.roll(part, 5, 0), 0.0))
            x_low = pltpu.roll(part, 3, 0)
            away.append(
                jnp.where(row < 3, 0.0, jnp.where(row < 6, x_low, jnp.where(row == 6, one, 0.0)))
            )
            spread.append(jnp.where(row < 3, -2.0 * part, jnp.where(row == 7, one, 0.0)))
        consts = []
        for f in (6, 7):
            h, m, l = (part[f : f + 1, :] for part in parts)
            consts.append(
                jnp.where(row == 0, h, jnp.where(row == 1, m, jnp.where(row == 2, l, 0.0)))
            )
        for k, (w, c) in enumerate(((facing, consts[0]), (away, zero), (spread, consts[1]))):
            h, m, l = w
            wtab[r, :, k * LANES : (k + 1) * LANES] = jnp.concatenate(
                [h, m, h, l, h, m, c, zero], 0
            ).astype(BF16)
        return 0

    lax.fori_loop(0, n_row * tiles, recv_body, 0, unroll=8)
    wone[...] = jnp.concatenate([zero] * 7 + [ones3], 0).astype(BF16)

    def emit_body(g, _):
        base = g * 9 * tiles
        for k in range(tiles):
            block = emit[pl.ds(pl.multiple_of(base + k * 8, 8), 8), :]
            h, m, l = split3(block)
            th, tm, tl = split3(emit[pl.ds(base + 8 * tiles + k, 1), :])
            tail = jnp.where(
                row == 0, th, jnp.where(row == 1, tm, jnp.where(row == 2, tl, 0.0))
            )
            etab[g * tiles + k] = jnp.concatenate([h, h, m, h, l, m, ones3, tail], 0).astype(BF16)
        return 0

    lax.fori_loop(0, n_col, emit_body, 0)
    acc[...] = jnp.zeros_like(acc)
    live = count[0]

    def fold(full):
        total = full[0:8]
        for k in range(1, LANES // 8):
            total = total + full[8 * k : 8 * k + 8]
        return total

    def pair(at):
        r = recv_list[at]
        e = emit_list[at]
        weights = jnp.concatenate([wtab[r], wone[...]], 1)
        g = lax.dot_general(etab[e], weights, TN, preferred_element_type=F32)
        facing = jnp.maximum(g[:, :LANES], 0.0)
        away = jnp.maximum(g[:, LANES : 2 * LANES], 0.0)
        spread = g[:, 2 * LANES : 3 * LANES]
        first = facing * away / (spread * spread)
        second = first * g[:, 3 * LANES :]
        return r, fold(first), fold(second)

    def step(i, _):
        found = [pair(i * unroll + k) for k in range(unroll)]
        for k, (r, first, second) in enumerate(found):
            keep = jnp.where(i * unroll + k < live, 1.0, 0.0)
            at = pl.multiple_of(r * 16, 16)
            acc[pl.ds(at, 8), :] = acc[pl.ds(at, 8), :] + first * keep
            acc[pl.ds(at + 8, 8), :] = acc[pl.ds(at + 8, 8), :] + second * keep
        return 0

    lax.fori_loop(0, (live + unroll - 1) // unroll, step, 0)
    for q in range(n_row):
        for v in range(2):
            total = acc[pl.ds(q * tiles * 16 + v * 8, tiles, stride=16), :]
            for s in range(1, 8):
                total = total + acc[pl.ds(q * tiles * 16 + v * 8 + s, tiles, stride=16), :]
            out[q * 2 * tiles + v * tiles : q * 2 * tiles + (v + 1) * tiles, :] = total


def load_kernel(tiles, n_row, part, basis, mirrored, inner, area, owner, rank, slots, gram, message, damped):
    sub = lax.broadcasted_iota(jnp.int32, (LANES, LANES), 0)
    irradiance = part[0:tiles, :]
    scattered = part[tiles : 2 * tiles, :]
    for q in range(1, n_row):
        irradiance = irradiance + part[2 * q * tiles : (2 * q + 1) * tiles, :]
        scattered = scattered + part[(2 * q + 1) * tiles : (2 * q + 2) * tiles, :]
    fraction = mirrored[...]
    lost = fraction * scattered
    damped[...] = lost
    power = (1.0 - fraction) * irradiance + inner[...]
    load = 20.0 * area[...] * jnp.sqrt(jnp.sqrt(power))
    parts = split3(load)
    found = jnp.zeros((LANES, LANES), F32)
    for g in range(tiles):
        hot = jnp.where(owner[g : g + 1, :] == sub, 1.0, 0.0).astype(BF16)
        at = rank[g : g + 1, :] == sub
        table = jnp.concatenate([jnp.where(at, v[g : g + 1, :], 0.0) for v in parts], 1)
        found = found + lax.dot_general(
            jnp.concatenate([hot] * 3, 1), table.astype(BF16), NT, preferred_element_type=F32
        )
    lanes = lax.broadcasted_iota(jnp.int32, (1, LANES), 1)
    stats = jnp.zeros((1, LANES), F32)
    for k in range(9):
        other = basis[k * tiles : (k + 1) * tiles, :] if k < 8 else lost
        value = jnp.sum(other * lost, axis=(0, 1), keepdims=True)
        stats = stats + jnp.where(lanes == 96 + k, value, 0.0)
    g = gram[...]
    shifted = pltpu.roll(jnp.broadcast_to(g, (8, LANES)), 105, 1)[0:1]
    stats = jnp.where(lanes >= 105, shifted, stats)
    more = pltpu.roll(jnp.broadcast_to(g, (8, LANES)), 73, 1)[0:1]
    keep = lax.broadcasted_iota(jnp.int32, (LANES, LANES), 1) < 96
    message[pl.ds(0, LANES, stride=2), :] = jnp.where(keep, found, stats)
    message[pl.ds(1, LANES, stride=2), :] = jnp.where(keep, slots[...], more)


def finish_kernel(tiles, cells, arrived, basis, damped, vector, hessen, loads, value_rows, index_rows):
    values = arrived[pl.ds(0, LANES, stride=2), :]
    second = arrived[pl.ds(1, LANES, stride=2), :]
    top = jnp.sum(values, axis=0, keepdims=True)
    low = jnp.sum(second, axis=0, keepdims=True)
    inner = [top[:, 96 + k : 97 + k] for k in range(8)]
    lost_square = top[:, 104:105]
    gram = {}
    at = 0
    for i in range(8):
        for j in range(i, 8):
            lane = 105 + at
            gram[i, j] = top[:, lane : lane + 1] if lane < 128 else low[:, lane - 32 : lane - 31]
            gram[j, i] = gram[i, j]
            at += 1
    scale = 1.0 / cells
    coeffs = [(gram[7, k] - inner[k]) * scale for k in range(8)]
    left = [(1.0 if k == 7 else 0.0) - coeffs[k] for k in range(8)]
    square = lost_square
    for i in range(8):
        line = gram[i, i] * left[i] - 2.0 * inner[i]
        for j in range(i + 1, 8):
            line = line + 2.0 * gram[i, j] * left[j]
        square = square + line * left[i]
    length = jnp.sqrt(jnp.maximum(square, 0.0) * scale + 1e-6)
    remainder = -damped[...]
    for k in range(8):
        remainder = remainder + left[k] * basis[k * tiles : (k + 1) * tiles, :]
    vector[...] = remainder / length
    lanes = lax.broadcasted_iota(jnp.int32, (1, LANES), 1)
    column = jnp.where(lanes == 8, length, 0.0)
    for k in range(8):
        column = column + jnp.where(lanes == k, coeffs[k], 0.0)
    hessen[...] = column
    keep = lax.broadcasted_iota(jnp.int32, (LANES, LANES), 1) < 96
    for k, v in enumerate(split3(jnp.where(keep, values, 0.0))):
        value_rows[k] = v
    index_rows[...] = second.astype(jnp.int32)
    sub = lax.broadcasted_iota(jnp.int32, (LANES, LANES), 0)
    sub16 = lax.broadcasted_iota(jnp.int32, (16, LANES), 0)
    total = jnp.zeros((48, LANES), F32)
    for s in range(0, LANES, 2):
        left_side, right_side = [], []
        for u in (s, s + 1):
            index = index_rows[u : u + 1, :]
            mask = (index >> 7) == sub16
            left_side.append(
                jnp.concatenate(
                    [jnp.where(mask, value_rows[k, u : u + 1, :], 0.0) for k in range(3)], 0
                ).astype(BF16)
            )
            right_side.append(jnp.where((index & 127) == sub, 1.0, 0.0).astype(BF16))
        total = total + lax.dot_general(
            jnp.concatenate(left_side, 1),
            jnp.concatenate(right_side, 1),
            NT,
            preferred_element_type=F32,
        )
    loads[...] = total[0:16] + total[16:32] + total[32:48]


def shards(
    positions,
    normals,
    patch_extents,
    mirrored_fraction,
    inner_emission_power,
    radiosity,
    basis,
    recv_blocks,
    emit_blocks,
    vis_count,
    owner,
    local_elem,
):
    patches = positions.shape[1]
    tiles = patches // LANES
    n_row, n_col = lax.axis_size("row"), lax.axis_size("col")
    devices = n_row * n_col
    shape = jax.ShapeDtypeStruct

    def rows(array):
        return array.reshape(-1, LANES)

    area = rows(patch_extents)
    basis_rows = rows(basis)
    emit, recv = call(
        functools.partial(stage_kernel, tiles, n_col, n_row),
        (shape((n_col * 9 * tiles, LANES), F32), shape((n_row * 8 * tiles, LANES), F32)),
        in_specs=[VMEM] * 5,
        name="stage",
    )(rows(positions), rows(normals), area, rows(radiosity), basis_rows[7 * tiles :])
    recv = lax.all_to_all(recv.reshape(n_row, -1), "row", 0, 0, tiled=True)
    emit = lax.all_to_all(emit.reshape(n_col, -1), "col", 0, 0, tiled=True)
    owner_rows = rows(owner)
    rank, slots, gram = call(
        functools.partial(rank_kernel, tiles),
        (shape((tiles, LANES), jnp.int32), shape((LANES, LANES), F32), shape((1, LANES), F32)),
        in_specs=[VMEM] * 3,
        name="rank",
    )(owner_rows, rows(local_elem), basis_rows)
    unroll = 16
    part = call(
        functools.partial(pair_kernel, tiles, n_row, n_col, unroll),
        shape((n_row * 2 * tiles, LANES), F32),
        scratch=[
            pltpu.VMEM((n_col * tiles, 64, LANES), BF16),
            pltpu.VMEM((n_row * tiles, 64, 3 * LANES), BF16),
            pltpu.VMEM((64, LANES), BF16),
            pltpu.VMEM((n_row * tiles * 16, LANES), F32),
        ],
        in_specs=[SMEM] * 3 + [VMEM] * 2,
        name="pairs",
    )(vis_count.reshape(-1), recv_blocks.reshape(-1), emit_blocks.reshape(-1), rows(emit), rows(recv))
    part = lax.all_to_all(part.reshape(n_row, -1), "row", 0, 0, tiled=True)
    message, damped = call(
        functools.partial(load_kernel, tiles, n_row),
        (shape((2 * devices, LANES), F32), shape((tiles, LANES), F32)),
        in_specs=[VMEM] * 9,
        name="loads",
    )(
        rows(part),
        basis_rows,
        rows(mirrored_fraction),
        rows(inner_emission_power),
        area,
        owner_rows,
        rank,
        slots,
        gram,
    )
    arrived = lax.all_to_all(message.reshape(devices, -1), ("row", "col"), 0, 0, tiled=True)
    vector, hessen, loads = call(
        functools.partial(finish_kernel, tiles, float(patches * devices)),
        (
            shape((tiles, LANES), F32),
            shape((1, LANES), F32),
            shape((E_DEV // LANES, LANES), F32),
        ),
        scratch=[pltpu.VMEM((3, LANES, LANES), F32), pltpu.VMEM((LANES, LANES), jnp.int32)],
        in_specs=[VMEM] * 3,
        name="finish",
    )(rows(arrived), basis_rows, damped)
    return vector.reshape(-1), hessen.reshape(-1)[:9], loads.reshape(-1)


def solution(mesh):
    in_specs = (
        P(None, ("row", "col")),
        P(None, ("row", "col")),
        P(("row", "col")),
        P(("row", "col")),
        P(("row", "col")),
        P(("row", "col")),
        P(None, ("row", "col")),
        P("row", "col", None),
        P("row", "col", None),
        P("row", "col"),
        P(("row", "col"), None),
        P(("row", "col")),
    )
    out_specs = (P(("row", "col")), P(), P(("row", "col")))
    return jax.shard_map(shards, mesh=mesh, in_specs=in_specs, out_specs=out_specs, check_vma=False)
```

time: 689 us -> 116 us (0.17); the launches traced: 679 us -> 115 us
  other arithmetic: 218 us -> 0 us
  local copies, waits for them, and re-layouts: 135 us -> 5.79 us
  blocking collectives: 157 us -> 37.3 us
  matrix products: 63.1 us -> 0 us
  waiting for transfers between devices: 73.5 us -> 28.6 us
  Pallas kernels: 0 us -> 22.2 us
  between operations: 15.6 us -> 1.46 us
  starting transfers between devices: 12.1 us -> 19.4 us
    psum x2 -> x0, blocking collectives: 132 us -> none  [the longest x1 69.1 us: shards(): lax.psum(jnp.dot(basis, applied, precision=lax.Precision.HIGHEST), ('row'...]
    scatter-add x33 -> x0, other arithmetic: 109 us -> none  [the longest x1 73.8 us: shards(): jnp.zeros((E_DEV,), jnp.float32).at[target_slots.reshape(-1)]]
    gather x64 -> x0, local copies, waits for them, and re-layouts: 72.2 us -> none  [the longest x32 54.1 us: group_sum(): recv_part = jnp.take(recv_tiles, receiver_selection, axis=1)]
    reduce_sum x34 -> x0, other arithmetic: 72.1 us -> none  [the longest x32 69.1 us: view_terms(): jnp.sum(receiver[3:6, :, :, None] * offset, axis=0)]
    dot_general x34 -> x0, matrix products: 63.1 us -> none  [the longest x32 60.8 us: view_terms(): jnp.einsum('gre,kge->kgr', factor, vectors, precision=lax.Precision.HIGHEST)]
    all_to_all x0 -> x2, blocking collectives: none -> 37.3 us  [the longest x1 20.1 us: shards(): lax.all_to_all(message.reshape(devices, -1), ('row', 'col'), 0, 0, tiled=...]
    psum x1 -> x0, waiting for transfers between devices: 36.1 us -> none  [shards(): summed = lax.psum(totals, 'row')]
    and x32 -> x0, other arithmetic: 25 us -> none  [group_sum(): recv_part = jnp.take(recv_tiles, receiver_selection, axis=1)]
  transfers between devices with their start and end apart: 4 -> 2, of which waited for: 4 -> 2; matrix products, arithmetic and copies ran while one was open for 3% -> 0% of each run, Pallas kernels for 0% -> 1%
where the time goes in v1:
time: 116 us; the launch traced here: 115 us
  blocking collectives  37.3 us (32%)
  waiting for transfers between devices  28.6 us (25%)
  Pallas kernels  22.2 us (19%)
  starting transfers between devices  19.4 us (17%)
  local copies, waits for them, and re-layouts  5.79 us (5%)
  between operations  1.46 us (1%)
    all_to_all x1, waiting for transfers between devices, shards(): emit = lax.all_to_all(emit.reshape(n_col, -1), 'col', 0, 0, tiled=True)  24.2 us
    all_to_all x1, blocking collectives, shards(): lax.all_to_all(message.reshape(devices, -1), ('row', 'col'), 0, 0, tiled=...  20.1 us
    all_to_all x1, blocking collectives, shards(): recv = lax.all_to_all(recv.reshape(n_row, -1), 'row', 0, 0, tiled=True)  17.2 us
    pallas_call x1, Pallas kernels, shards(): call(functools.partial(pair_kernel, tiles, n_row, n_col, unroll), shape((...  17.2 us
    all_to_all x1, starting transfers between devices, shards(): emit = lax.all_to_all(emit.reshape(n_col, -1), 'col', 0, 0, tiled=True)  10 us
    all_to_all x1, starting transfers between devices, shards(): part = lax.all_to_all(part.reshape(n_row, -1), 'row', 0, 0, tiled=True)  9.41 us
    all_to_all x1, waiting for transfers between devices, shards(): part = lax.all_to_all(part.reshape(n_row, -1), 'row', 0, 0, tiled=True)  4.39 us
    unnamed x22, local copies, waits for them, and re-layouts  2.7 us
  transfers between devices with their start and end apart: 2, of which 2 were waited for; matrix products, arithmetic and copies ran while one was open for 0% of the time, Pallas kernels for 1%

profile of v1, /device:TPU:1, one launch (start us, length us, event | category | flops | bytes accessed | tf_op | source)
XLA Modules:
  0.0 114.8 jit_solution(13682666082000667402)
XLA Ops:
  0.6 0.8 reshape.86.pos
  1.5 0.8 reshape.87.nor
  2.3 0.9 slice.12
  3.2 0.0 copy-start.1
  3.2 0.7 copy-done.1
  3.9 0.0 copy-start.6
  3.9 0.7 copy-done.6
  4.6 0.6 stage.1
  5.2 0.0 copy-start
  5.2 1.3 %copy-done = f32[3456,128]{1,0:T(8,128)} copy-done((f32[3456,128]{1,0:T(8,128)}, f32[3456,128]{1,0:T(8,128)S(1)}, u32[]{:S(2)}) %copy-start) | copy-done | bytes 1769496
  6.4 17.2 %all_to_all.36 = f32[8,1,24576]{2,1,0:T(1,128)S(1)} all-to-all(f32[8,1,24576]{2,1,0:T(1,128)S(1)} %bitcast.26), channel_id=1, replica_groups=mesh['row'=8,'col'=16] {'row'}, dimensions={0} | all-to-all | bytes 1572864 | tf_op jit(solution)/shard_map/all_to_all | solution.py:314
  23.6 0.0 copy-start.8
  23.7 0.0 copy-start.9
  23.7 10.0 %all-to-all-start = ((f32[16,1,27648]{2,1,0:T(1,128)}), f32[16,1,27648]{2,1,0:T(1,128)S(1)}, u32[]{:S(2)}, u32[]{:S(2)}) async-start(f32[16,1,27648]{2,1,0:T(1,128)} %bitcast.25), calls=%async_computation | async-start | bytes 3538944 | tf_op jit(solution)/shard_map/all_to_all | solution.py:315
  33.7 0.0 copy-start.10
  33.7 0.0 copy-start.3
  33.7 0.0 copy-start.7
  33.7 0.0 copy-start.2
  33.7 0.0 copy-start.4
  33.7 0.0 copy-start.5
  34.5 24.2 %all-to-all-done = f32[16,1,27648]{2,1,0:T(1,128)S(1)} async-done(((f32[16,1,27648]{2,1,0:T(1,128)}), f32[16,1,27648]{2,1,0:T(1,128)S(1)}, u32[]{:S(2)}, u32[]{:S(2)}) %all-to-all-start) | async-done | bytes 1769504 | tf_op jit(solution)/shard_map/all_to_all | solution.py:315
  58.6 0.0 copy-done.8
  58.6 0.0 copy-done.9
  58.6 17.2 %pairs.1 = f32[384,128]{1,0:T(8,128)} custom-call(s32[1]{0:T(128)} %bitcast.22.count, s32[512]{0:T(512)S(1)} %bitcast.39, s32[512]{0:T(512)S(1)} %bitcast.40, f32[3456,128]{1,0:T(8,128)S(1)} %bitcast.23, f32[1536,128]{1,0:T(8,128)S(1)} %bitcast.24), custom_call_target="tpu_custom_call" | custom-call | tf_op jit(solution)/shard_map/pairs/pallas_call | solution.py:324
  75.8 9.4 %all-to-all-start.2 = ((f32[8,1,6144]{2,1,0:T(1,128)}), f32[8,1,6144]{2,1,0:T(1,128)S(1)}, u32[]{:S(2)}, u32[]{:S(2)}) async-start(f32[8,1,6144]{2,1,0:T(1,128)} %bitcast.10), calls=%async_computation.2 | async-start | bytes 393216 | tf_op jit(solution)/shard_map/all_to_all | solution.py:336
  85.2 0.0 copy-done.10
  85.2 0.0 copy-done.3
  85.3 0.0 copy-done.7
  85.3 1.3 %rank.1 = (s32[24,128]{1,0:T(8,128)S(1)}, f32[128,128]{1,0:T(8,128)S(1)}, f32[1,128]{1,0:T(1,128)S(1)}) custom-call(s32[24,128]{1,0:T(8,128)S(1)} %bitcast.32, s32[24,128]{1,0:T(8,128)S(1)} %bitcast.38, f32[192,128]{1,0:T(8,128)S(1)} %reshape.93.basis), custom_call_target="tpu_custom_call" | custom-call | tf_op jit(solution)/shard_map/rank/pallas_call | solution.py:317
  86.6 4.4 %all-to-all-done.2 = f32[8,1,6144]{2,1,0:T(1,128)S(1)} async-done(((f32[8,1,6144]{2,1,0:T(1,128)}), f32[8,1,6144]{2,1,0:T(1,128)S(1)}, u32[]{:S(2)}, u32[]{:S(2)}) %all-to-all-start.2) | async-done | bytes 196640 | tf_op jit(solution)/shard_map/all_to_all | solution.py:336
  91.0 0.0 copy-done.2
  91.0 0.0 copy-done.4
  91.0 0.0 copy-done.5
  91.0 1.1 loads.1
  92.2 20.1 %all_to_all.37 = f32[128,1,256]{2,1,0:T(1,128)S(1)} all-to-all(f32[128,1,256]{2,1,0:T(1,128)S(1)} %bitcast.29), channel_id=1, replica_groups=mesh['row'=8,'col'=16] {'row','col'}, dimensions={0} | all-to-all | bytes 262144 | tf_op jit(solution)/shard_map/all_to_all | solution.py:353
  112.3 2.0 %finish.1 = (f32[24,128]{1,0:T(8,128)}, f32[1,128]{1,0:T(1,128)S(1)}, f32[16,128]{1,0:T(8,128)}) custom-call(f32[256,128]{1,0:T(8,128)S(1)} %bitcast.28, f32[192,128]{1,0:T(8,128)S(1)} %reshape.93.basis, f32[24,128]{1,0:T(8,128)S(1)} %get-tuple-element.19.damped), custom_call_target="tpu_custom_call" | custom-call | tf_op jit(solution)/shard_map/finish/pallas_call | solution.py:354
  114.3 0.5 slice_bitcast_fusion
  (1 shorter events, 0.0 us)
Async XLA Ops:
  3.2 0.7 copy-start.1
  3.9 0.7 copy-start.6
  5.2 1.3 %copy-start = (f32[3456,128]{1,0:T(8,128)}, f32[3456,128]{1,0:T(8,128)S(1)}, u32[]{:S(2)}) copy-start(f32[3456,128]{1,0:T(8,128)S(1)} %get-tuple-element.13) | copy-start | bytes 5308420
  23.6 35.0 %copy-start.8 = (s32[1,1,512]{2,1,0:T(1,128)S(1)}, s32[1,1,512]{2,1,0:T(1,128)}, u32[]{:S(2)}) copy-start(s32[1,1,512]{2,1,0:T(1,128)} %param.19) | copy-start | bytes 6148
  23.7 35.0 %copy-start.9 = (s32[1,1,512]{2,1,0:T(1,128)S(1)}, s32[1,1,512]{2,1,0:T(1,128)}, u32[]{:S(2)}) copy-start(s32[1,1,512]{2,1,0:T(1,128)} %param.20) | copy-start | bytes 6148
  23.7 35.0 %all-to-all-start = ((f32[16,1,27648]{2,1,0:T(1,128)}), f32[16,1,27648]{2,1,0:T(1,128)S(1)}, u32[]{:S(2)}, u32[]{:S(2)}) async-start(f32[16,1,27648]{2,1,0:T(1,128)} %bitcast.25), calls=%async_computation | async-start | bytes 3538944 | tf_op jit(solution)/shard_map/all_to_all | solution.py:315
  33.7 51.5 %copy-start.10 = (f32[8,3072]{1,0:T(8,128)S(1)}, f32[8,3072]{1,0:T(8,128)}, u32[]{:S(2)}) copy-start(f32[8,3072]{1,0:T(8,128)} %param.18) | copy-start | bytes 294916
  33.7 51.6 %copy-start.3 = (s32[3072,1]{0,1:T(1,128)S(1)}, s32[3072,1]{0,1:T(1,128)}, u32[]{:S(2)}) copy-start(s32[3072,1]{0,1:T(1,128)} %param.22) | copy-start | bytes 36868
  33.7 51.6 %copy-start.7 = (s32[3072]{0:T(1024)S(1)}, s32[3072]{0:T(1024)}, u32[]{:S(2)}) copy-start(s32[3072]{0:T(1024)} %param.23) | copy-start | bytes 36868
  33.7 57.3 %copy-start.2 = (f32[3072]{0:T(1024)S(1)}, f32[3072]{0:T(1024)}, u32[]{:S(2)}) copy-start(f32[3072]{0:T(1024)} %param.14) | copy-start | bytes 36868
  33.7 57.3 %copy-start.4 = (f32[3072]{0:T(1024)S(1)}, f32[3072]{0:T(1024)}, u32[]{:S(2)}) copy-start(f32[3072]{0:T(1024)} %param.15) | copy-start | bytes 36868
  33.7 57.3 %copy-start.5 = (f32[3072]{0:T(1024)S(1)}, f32[3072]{0:T(1024)}, u32[]{:S(2)}) copy-start(f32[3072]{0:T(1024)} %param.16) | copy-start | bytes 36868
  75.8 15.2 %all-to-all-start.2 = ((f32[8,1,6144]{2,1,0:T(1,128)}), f32[8,1,6144]{2,1,0:T(1,128)S(1)}, u32[]{:S(2)}, u32[]{:S(2)}) async-start(f32[8,1,6144]{2,1,0:T(1,128)} %bitcast.10), calls=%async_computation.2 | async-start | bytes 393216 | tf_op jit(solution)/shard_map/all_to_all | solution.py:336

commit v2 on v1

v2 whole, which is shorter than its diff:
```python
import functools
import math

import jax
import jax.numpy as jnp
from jax import lax
from jax.experimental import pallas as pl
from jax.experimental.pallas import tpu as pltpu
from jax.sharding import Mesh, PartitionSpec as P

F32 = jnp.float32
BF16 = jnp.bfloat16
LANES = 128
AXES = ("pair", "ring", "half", "core")
ROW = ("pair", "ring")
E_DEV = 2048
NT = (((1,), (1,)), ((), ()))
TN = (((0,), (0,)), ((), ()))
VMEM = pl.BlockSpec(memory_space=pltpu.VMEM)
SMEM = pl.BlockSpec(memory_space=pltpu.SMEM)
LIMIT = 32 * 2**20


def split3(value):
    high = value.astype(BF16).astype(F32)
    rest = value - high
    middle = rest.astype(BF16).astype(F32)
    return high, middle, rest - middle


def call(body, out_shape, scratch=(), in_specs=None, name=None, micros=1, limit=LIMIT):
    return pl.pallas_call(
        body,
        out_shape=out_shape,
        in_specs=in_specs,
        out_specs=jax.tree.map(lambda _: VMEM, out_shape),
        scratch_shapes=list(scratch),
        compiler_params=pltpu.CompilerParams(vmem_limit_bytes=limit),
        cost_estimate=pl.CostEstimate(
            flops=int(micros * 1.1e9), bytes_accessed=2**16, transcendentals=0
        ),
        name=name,
    )


def stage_kernel(tiles, copies, pos, nor, area, rad, basis, emit, recv, pos_v, nor_v, area_v, rad_v, last_v, sems):
    moves = [
        pltpu.make_async_copy(source, target, sems.at[k])
        for k, (source, target) in enumerate(
            (
                (pos, pos_v),
                (nor, nor_v),
                (area, area_v),
                (rad, rad_v),
                (basis, last_v),
            )
        )
    ]
    for move in moves:
        move.start()
    for move in moves:
        move.wait()
    x = pos_v[...]
    n = nor_v[...]
    a = area_v[...]
    b = rad_v[...]
    m = (a * b * (1.0 / math.pi)) * n
    product = n * x
    square = x * x
    square = square[0:1] + square[1:2] + square[2:3]
    along = product[0:1] + product[1:2] + product[2:3]
    emit_rows = jnp.concatenate([x, m, square + a, last_v[7:8, :] / b], 0)
    recv_rows = jnp.concatenate([x, n, -along, square], 0)
    for k in range(tiles):
        block = emit_rows[:, k * LANES : (k + 1) * LANES]
        for c in range(copies):
            emit[(c * tiles + k) * 8 : (c * tiles + k + 1) * 8, :] = block
        recv[k * 8 : (k + 1) * 8, :] = recv_rows[:, k * LANES : (k + 1) * LANES]


def rank_kernel(tiles, n_row, n_col, place, owner, elem, basis, recv_list, emit_list, rank, slots, gram, recv_at, emit_at):
    my_pair, my_ring, my_core = place[0], place[1], place[2]
    ring = n_row // 2
    step_of = -(-65536 // tiles)
    r = recv_list[...]
    q = (r * step_of) >> 16
    side = (q >= ring).astype(jnp.int32) ^ my_pair
    recv_at[...] = (((my_ring - q) & (ring - 1)) * 2 + side) * tiles + r - q * tiles
    e = emit_list[...]
    c = (e * step_of) >> 16
    emit_at[...] = ((c >> 1) + ((c ^ my_core) & 1) * (n_col // 2)) * tiles + e - c * tiles
    sub = lax.broadcasted_iota(jnp.int32, (LANES, LANES), 0)
    lane = lax.broadcasted_iota(jnp.int32, (LANES, LANES), 1)
    upper = jnp.concatenate([(sub < lane).astype(BF16), jnp.ones((LANES, LANES), BF16)], 1)
    carry = jnp.zeros((LANES, LANES), F32)
    found = jnp.zeros((LANES, 2 * LANES), F32)
    for g in range(tiles):
        named = owner[g : g + 1, :] == sub
        hot = jnp.where(named, 1.0, 0.0)
        counts = jnp.dot(hot.astype(BF16), upper, preferred_element_type=F32)
        place = jnp.sum(hot * (counts[:, :LANES] + carry), axis=0, keepdims=True)
        carry = carry + counts[:, LANES:]
        place = place.astype(jnp.int32)
        rank[g : g + 1, :] = place
        index = elem[g : g + 1, :]
        high = (index >> 7).astype(F32)
        low = (index & 127).astype(F32)
        at = place == sub
        table = jnp.concatenate([jnp.where(at, high, 0.0), jnp.where(at, low, 0.0)], 0)
        found = found + lax.dot_general(
            hot.astype(BF16), table.astype(BF16), NT, preferred_element_type=F32
        )
    slots[...] = found[:, :LANES] * 128.0 + found[:, LANES:]
    lanes = lax.broadcasted_iota(jnp.int32, (8, LANES), 1)
    subs = lax.broadcasted_iota(jnp.int32, (8, LANES), 0)
    total = jnp.zeros((8, LANES), F32)
    at = 0
    for i in range(8):
        sums = jnp.zeros((8, LANES), F32)
        for g in range(tiles):
            block = basis[:, g * LANES : (g + 1) * LANES]
            sums = sums + block * block[i : i + 1]
        value = jnp.sum(sums, axis=1, keepdims=True)
        total = total + jnp.where((subs >= i) & (lanes == at + subs - i), value, 0.0)
        at += 8 - i
    gram[...] = jnp.sum(total, axis=0, keepdims=True)


def receiver_kernel(*refs):
    wtab = refs[-1]
    row = lax.broadcasted_iota(jnp.int32, (8, LANES), 0)
    zero = jnp.zeros((8, LANES), F32)
    base = 0
    for recv in refs[:-1]:
        blocks = recv.shape[0] // 8

        def body(k, _):
            block = recv[pl.ds(pl.multiple_of(k * 8, 8), 8), :]
            parts = split3(block)
            facing, away, spread = [], [], []
            for p, part in enumerate(parts):
                one = 1.0 if p == 0 else 0.0
                x_low = pltpu.roll(part, 3, 0)
                facing.append(jnp.where(row < 3, pltpu.roll(part, 5, 0), 0.0))
                away.append(jnp.where((row >= 3) & (row < 6), x_low, 0.0))
                spread.append(jnp.where(row < 3, -2.0 * part, jnp.where(row == 6, one, 0.0)))
            consts = []
            for f in (6, 7):
                h, m, l = (part[f : f + 1, :] for part in parts)
                consts.append(
                    jnp.where(row == 0, h, jnp.where(row == 1, m, jnp.where(row == 2, l, 0.0)))
                )
            ones = jnp.where((row >= 3) & (row < 6), 1.0, 0.0)
            for p, (w, c) in enumerate(
                ((facing, consts[0]), (away, ones), (spread, consts[1]))
            ):
                h, m, l = w
                wtab[base + k, :, p * LANES : (p + 1) * LANES] = jnp.concatenate(
                    [h, m, h, l, h, m, c, zero], 0
                ).astype(BF16)
            return 0

        lax.fori_loop(0, blocks, body, 0, unroll=8)
        base += blocks


def pair_kernel(tiles, n_row, n_col, unroll, count, recv_list, emit_list, place, near, far, wtab, out, etab, along, ratio, acc):
    row = lax.broadcasted_iota(jnp.int32, (8, LANES), 0)
    ones3 = jnp.where(row < 3, 1.0, 0.0)
    half = n_col // 2
    blocks = half * tiles
    ratios = []
    for s, source in enumerate((near, far)):
        feature = [source[pl.ds(f, blocks, stride=8), :] for f in range(8)]
        ratios.append(feature[7])
        total = -(feature[0] * feature[3] + feature[1] * feature[4] + feature[2] * feature[5])
        for p, part in enumerate(split3(total)):
            along[p, s * blocks : (s + 1) * blocks, :] = part
    ratios = jnp.concatenate(ratios, 0)
    for k in range(2 * blocks // LANES):
        ratio[k] = ratios[k * LANES : (k + 1) * LANES].T
    for s, source in enumerate((near, far)):

        def body(g, _):
            for k in range(tiles):
                at = g * tiles + k
                h, m, l = split3(source[pl.ds(pl.multiple_of(at * 8, 8), 8), :])
                ph, pm, pl_ = (along[p, pl.ds(s * blocks + at, 1), :] for p in range(3))
                tail = jnp.where(
                    row < 3,
                    1.0,
                    jnp.where(
                        row == 3, ph, jnp.where(row == 4, pm, jnp.where(row == 5, pl_, 0.0))
                    ),
                )
                etab[s * blocks + at] = jnp.concatenate(
                    [h, h, m, h, l, m, tail, jnp.zeros_like(tail)], 0
                ).astype(BF16)
            return 0

        lax.fori_loop(0, half, body, 0)
    acc[...] = jnp.zeros_like(acc)
    live = count[0]

    def fold(full):
        total = full[0:8]
        for k in range(1, LANES // 8):
            total = total + full[8 * k : 8 * k + 8]
        return total

    my_pair, my_ring = place[0], place[1]
    ring = n_row // 2

    def pair(at):
        r = recv_list[at]
        e = emit_list[at]
        g = lax.dot_general(etab[e], wtab[r], TN, preferred_element_type=F32)
        facing = jnp.maximum(g[:, :LANES], 0.0)
        away = jnp.maximum(g[:, LANES : 2 * LANES], 0.0)
        spread = g[:, 2 * LANES :]
        first = facing * away / (spread * spread)
        lane = jnp.full((LANES, LANES), e & (LANES - 1), jnp.int32)
        factor = jnp.take_along_axis(ratio[e >> 7], lane, axis=1, mode="promise_in_bounds")
        return r, fold(first), fold(first * factor)

    def step(i, _):
        found = [pair(i * unroll + k) for k in range(unroll)]
        for k, (r, first, second) in enumerate(found):
            keep = jnp.where(i * unroll + k < live, 1.0, 0.0)
            at = pl.multiple_of(r * 16, 16)
            acc[pl.ds(at, 8), :] = acc[pl.ds(at, 8), :] + first * keep
            acc[pl.ds(at + 8, 8), :] = acc[pl.ds(at + 8, 8), :] + second * keep
        return 0

    lax.fori_loop(0, (live + unroll - 1) // unroll, step, 0)
    for q in range(n_row):
        target = (my_pair ^ (q & 1)) * ring + ((my_ring - (q >> 1)) & (ring - 1))
        for v in range(2):
            total = acc[pl.ds(q * tiles * 16 + v * 8, tiles, stride=16), :]
            for s in range(1, 8):
                total = total + acc[pl.ds(q * tiles * 16 + v * 8 + s, tiles, stride=16), :]
            at = pl.multiple_of((target * 2 + v) * tiles, 8)
            out[pl.ds(at, tiles), :] = total


def load_kernel(tiles, n_row, part, basis, mirrored, inner, area, owner, rank, slots, gram, message, damped):
    sub = lax.broadcasted_iota(jnp.int32, (LANES, LANES), 0)
    irradiance = part[0:tiles, :]
    scattered = part[tiles : 2 * tiles, :]
    for q in range(1, n_row):
        irradiance = irradiance + part[2 * q * tiles : (2 * q + 1) * tiles, :]
        scattered = scattered + part[(2 * q + 1) * tiles : (2 * q + 2) * tiles, :]
    fraction = mirrored[...]
    lost = fraction * scattered
    damped[...] = lost
    power = (1.0 - fraction) * irradiance + inner[...]
    load = 20.0 * area[...] * jnp.sqrt(jnp.sqrt(power))
    parts = split3(load)
    found = jnp.zeros((LANES, LANES), F32)
    for g in range(tiles):
        hot = jnp.where(owner[g : g + 1, :] == sub, 1.0, 0.0).astype(BF16)
        at = rank[g : g + 1, :] == sub
        table = jnp.concatenate([jnp.where(at, v[g : g + 1, :], 0.0) for v in parts], 1)
        found = found + lax.dot_general(
            jnp.concatenate([hot] * 3, 1), table.astype(BF16), NT, preferred_element_type=F32
        )
    lanes = lax.broadcasted_iota(jnp.int32, (8, LANES), 1)
    subs = lax.broadcasted_iota(jnp.int32, (8, LANES), 0)
    sums = jnp.zeros((8, LANES), F32)
    for g in range(tiles):
        sums = sums + basis[:, g * LANES : (g + 1) * LANES] * lost[g : g + 1, :]
    inner_products = jnp.sum(sums, axis=1, keepdims=True)
    square = jnp.sum(lost * lost, axis=(0, 1), keepdims=True)
    stats = jnp.sum(
        jnp.where(lanes == 96 + subs, inner_products, 0.0), axis=0, keepdims=True
    )
    g = jnp.broadcast_to(gram[...], (8, LANES))
    lane = lanes[0:1]
    stats = jnp.where(lane == 104, square, stats)
    stats = jnp.where(lane >= 105, pltpu.roll(g, 105, 1)[0:1], stats)
    more = pltpu.roll(g, 73, 1)[0:1]
    keep = lax.broadcasted_iota(jnp.int32, (LANES, LANES), 1) < 96
    message[pl.ds(0, LANES, stride=2), :] = jnp.where(keep, found, stats)
    message[pl.ds(1, LANES, stride=2), :] = jnp.where(keep, slots[...], more)


def finish_kernel(tiles, cells, arrived, basis, damped, vector, hessen, loads, value_rows, index_rows):
    values = arrived[pl.ds(0, LANES, stride=2), :]
    second = arrived[pl.ds(1, LANES, stride=2), :]
    top = jnp.sum(values, axis=0, keepdims=True)
    low = jnp.sum(second, axis=0, keepdims=True)
    inner = [top[:, 96 + k : 97 + k] for k in range(8)]
    lost_square = top[:, 104:105]
    gram = {}
    at = 0
    for i in range(8):
        for j in range(i, 8):
            lane = 105 + at
            gram[i, j] = top[:, lane : lane + 1] if lane < 128 else low[:, lane - 32 : lane - 31]
            gram[j, i] = gram[i, j]
            at += 1
    scale = 1.0 / cells
    coeffs = [(gram[7, k] - inner[k]) * scale for k in range(8)]
    left = [(1.0 if k == 7 else 0.0) - coeffs[k] for k in range(8)]
    square = lost_square
    for i in range(8):
        line = gram[i, i] * left[i] - 2.0 * inner[i]
        for j in range(i + 1, 8):
            line = line + 2.0 * gram[i, j] * left[j]
        square = square + line * left[i]
    length = jnp.sqrt(jnp.maximum(square, 0.0) * scale + 1e-6)
    subs = lax.broadcasted_iota(jnp.int32, (8, LANES), 0)
    weights = jnp.zeros((8, LANES), F32)
    for k in range(8):
        weights = jnp.where(subs == k, left[k], weights)
    for g in range(tiles):
        mixed = jnp.sum(basis[:, g * LANES : (g + 1) * LANES] * weights, axis=0, keepdims=True)
        vector[g : g + 1, :] = (mixed - damped[g : g + 1, :]) / length
    lanes = lax.broadcasted_iota(jnp.int32, (1, LANES), 1)
    column = jnp.where(lanes == 8, length, 0.0)
    for k in range(8):
        column = jnp.where(lanes == k, coeffs[k], column)
    hessen[...] = column[:, 0:9]
    keep = lax.broadcasted_iota(jnp.int32, (LANES, LANES), 1) < 96
    for k, v in enumerate(split3(jnp.where(keep, values, 0.0))):
        value_rows[k] = v
    index_rows[...] = second.astype(jnp.int32)
    sub = lax.broadcasted_iota(jnp.int32, (LANES, LANES), 0)
    sub16 = lax.broadcasted_iota(jnp.int32, (16, LANES), 0)
    total = jnp.zeros((48, LANES), F32)
    for s in range(0, LANES, 2):
        left_side, right_side = [], []
        for u in (s, s + 1):
            index = index_rows[u : u + 1, :]
            mask = (index >> 7) == sub16
            left_side.append(
                jnp.concatenate(
                    [jnp.where(mask, value_rows[k, u : u + 1, :], 0.0) for k in range(3)], 0
                ).astype(BF16)
            )
            right_side.append(jnp.where((index & 127) == sub, 1.0, 0.0).astype(BF16))
        total = total + lax.dot_general(
            jnp.concatenate(left_side, 1),
            jnp.concatenate(right_side, 1),
            NT,
            preferred_element_type=F32,
        )
    loads[...] = total[0:16] + total[16:32] + total[32:48]


def shards(
    positions,
    normals,
    patch_extents,
    mirrored_fraction,
    inner_emission_power,
    radiosity,
    basis,
    recv_blocks,
    emit_blocks,
    vis_count,
    owner,
    local_elem,
):
    patches = positions.shape[1]
    tiles = patches // LANES
    pairs_of, ring, half, cores = (lax.axis_size(a) for a in AXES)
    n_row, n_col = pairs_of * ring, half * cores
    devices = n_row * n_col
    place = jnp.stack([lax.axis_index(a) for a in ("pair", "ring", "core")])
    shape = jax.ShapeDtypeStruct

    def rows(array):
        return array.reshape(-1, LANES)

    emit, recv = call(
        functools.partial(stage_kernel, tiles, half),
        (shape((half * 8 * tiles, LANES), F32), shape((8 * tiles, LANES), F32)),
        scratch=[
            pltpu.VMEM((3, patches), F32),
            pltpu.VMEM((3, patches), F32),
            pltpu.VMEM((1, patches), F32),
            pltpu.VMEM((1, patches), F32),
            pltpu.VMEM((8, patches), F32),
            pltpu.SemaphoreType.DMA((5,)),
        ],
        in_specs=[pl.BlockSpec(memory_space=pl.ANY)] * 5,
        name="stage",
        limit=60 * 2**20,
    )(positions, normals, patch_extents[None], radiosity[None], basis)
    swapped = lax.ppermute(recv, "pair", [(0, 1), (1, 0)])
    emit, swapped = lax.optimization_barrier((emit, swapped))
    both = jnp.concatenate([recv, swapped], 0)
    owner_rows, both_again = lax.optimization_barrier((rows(owner), both))
    lists = rows(recv_blocks), rows(emit_blocks)
    rank, slots, gram, recv_at, emit_at = call(
        functools.partial(rank_kernel, tiles, n_row, n_col),
        (
            shape((tiles, LANES), jnp.int32),
            shape((LANES, LANES), F32),
            shape((1, LANES), F32),
            shape(lists[0].shape, jnp.int32),
            shape(lists[1].shape, jnp.int32),
        ),
        in_specs=[SMEM] + [VMEM] * 5,
        name="rank",
        micros=20,
        limit=60 * 2**20,
    )(place, owner_rows, rows(local_elem), basis, *lists)
    received = [both_again] + [
        lax.ppermute(both, "ring", [(i, (i + k) % ring) for i in range(ring)])
        for k in range(1, ring)
    ]
    near = rows(lax.all_to_all(emit.reshape(half, -1), "half", 0, 0, tiled=True))
    near, received, recv_at, emit_at = lax.optimization_barrier(
        (near, received, recv_at, emit_at)
    )
    far = lax.ppermute(near, "core", [(0, 1), (1, 0)])
    wtab = call(
        receiver_kernel,
        shape((n_row * tiles, 64, 3 * LANES), BF16),
        in_specs=[VMEM] * len(received),
        name="receivers",
        micros=4,
    )(*received)
    unroll = 32
    part = call(
        functools.partial(pair_kernel, tiles, n_row, n_col, unroll),
        shape((n_row * 2 * tiles, LANES), F32),
        scratch=[
            pltpu.VMEM((n_col * tiles, 64, LANES), BF16),
            pltpu.VMEM((3, n_col * tiles, LANES), F32),
            pltpu.VMEM((n_col * tiles // LANES, LANES, LANES), F32),
            pltpu.VMEM((n_row * tiles * 16, LANES), F32),
        ],
        in_specs=[SMEM] * 4 + [VMEM] * 3,
        name="pairs",
        micros=20,
    )(
        vis_count.reshape(-1),
        recv_at.reshape(-1),
        emit_at.reshape(-1),
        place,
        near,
        far,
        wtab,
    )
    part = lax.all_to_all(part.reshape(n_row, -1), ROW, 0, 0, tiled=True)
    message, damped = call(
        functools.partial(load_kernel, tiles, n_row),
        (shape((2 * devices, LANES), F32), shape((tiles, LANES), F32)),
        in_specs=[VMEM] * 9,
        name="loads",
    )(
        rows(part),
        basis,
        rows(mirrored_fraction),
        rows(inner_emission_power),
        rows(patch_extents),
        owner_rows,
        rank,
        slots,
        gram,
    )
    arrived = lax.all_to_all(message.reshape(devices, -1), AXES, 0, 0, tiled=True)
    vector, hessen, loads = call(
        functools.partial(finish_kernel, tiles, float(patches * devices)),
        (
            shape((tiles, LANES), F32),
            shape((1, 9), F32),
            shape((E_DEV // LANES, LANES), F32),
        ),
        scratch=[pltpu.VMEM((3, LANES, LANES), F32), pltpu.VMEM((LANES, LANES), jnp.int32)],
        in_specs=[VMEM] * 3,
        name="finish",
    )(rows(arrived), basis, damped)
    return vector.reshape(-1), hessen.reshape(-1), loads.reshape(-1)


def solution(mesh):
    n_row, n_col = mesh.shape["row"], mesh.shape["col"]
    fine = Mesh(mesh.devices.reshape(2, n_row // 2, n_col // 2, 2), AXES)
    every = P(AXES)
    second = P(None, AXES)
    grid = P(ROW, ("half", "core"))
    in_specs = (
        second,
        second,
        every,
        every,
        every,
        every,
        second,
        P(ROW, ("half", "core"), None),
        P(ROW, ("half", "core"), None),
        grid,
        P(AXES, None),
        every,
    )
    return jax.shard_map(
        shards, mesh=fine, in_specs=in_specs, out_specs=(every, P(), every), check_vma=False
    )
```

time: 116 us -> 82.6 us (0.71)
  waiting for transfers between devices: 28.6 us -> 7.64 us
  blocking collectives: 37.3 us -> 31.2 us
  local copies, waits for them, and re-layouts: 5.79 us -> 1 us
  Pallas kernels: 22.2 us -> 20.5 us
    all_to_all x2 -> x1, waiting for transfers between devices: 28.6 us -> 6.92 us  [shards(): lax.all_to_all(emit.reshape(half, -1), 'half', 0, 0, tiled=True)]
    ppermute x0 -> x5, starting transfers between devices: none -> 12.1 us  [the longest x3 5.3 us: shards(): lax.ppermute(both, 'ring', [(i, (i + k) % ring) for i in range(ring)])]
    all_to_all x2 -> x1, starting transfers between devices: 19.4 us -> 7.49 us  [shards(): lax.all_to_all(emit.reshape(half, -1), 'half', 0, 0, tiled=True)]
    pallas_call x1, Pallas kernels: 17.2 us -> 10.9 us  [shards(): call(functools.partial(pair_kernel, tiles, n_row, n_col, unroll), shape((...]
    all_to_all x2, blocking collectives: 37.3 us -> 31.2 us  [the longest x1 15.6 us: shards(): lax.all_to_all(message.reshape(devices, -1), AXES, 0, 0, tiled=True)]
    pallas_call x2 -> x3, Pallas kernels: 1.91 us -> 6.46 us  [the longest x1 2.92 us: shards(): call(functools.partial(rank_kernel, tiles, n_row, n_col), (shape((tiles,...]
    unnamed x22 -> x23, local copies, waits for them, and re-layouts: 2.7 us -> 0.99 us
    reshape x3 -> x0, local copies, waits for them, and re-layouts: 1.66 us -> none  [rows(): return array.reshape(-1, LANES)]
  transfers between devices with their start and end apart: 2 -> 6, of which waited for: 2 -> 2; matrix products, arithmetic and copies ran while one was open for 0% -> 2% of each run, Pallas kernels for 1% -> 5%
where the time goes in v2:
time: 82.6 us; the launch traced here: 82.1 us
  blocking collectives  31.2 us (38%)
  Pallas kernels  20.5 us (25%)
  starting transfers between devices  19.6 us (24%)
  waiting for transfers between devices  7.64 us (9%)
  between operations  1.49 us (2%)
  local copies, waits for them, and re-layouts  1 us (1%)
    all_to_all x1, blocking collectives, shards(): lax.all_to_all(message.reshape(devices, -1), AXES, 0, 0, tiled=True)  15.6 us
    all_to_all x1, blocking collectives, shards(): part = lax.all_to_all(part.reshape(n_row, -1), ROW, 0, 0, tiled=True)  15.6 us
    pallas_call x1, Pallas kernels, shards(): call(functools.partial(pair_kernel, tiles, n_row, n_col, unroll), shape((...  10.9 us
    all_to_all x1, starting transfers between devices, shards(): lax.all_to_all(emit.reshape(half, -1), 'half', 0, 0, tiled=True)  7.49 us
    all_to_all x1, waiting for transfers between devices, shards(): lax.all_to_all(emit.reshape(half, -1), 'half', 0, 0, tiled=True)  6.92 us
    ppermute x3, starting transfers between devices, shards(): lax.ppermute(both, 'ring', [(i, (i + k) % ring) for i in range(ring)])  5.3 us
    ppermute x1, starting transfers between devices, shards(): far = lax.ppermute(near, 'core', [(0, 1), (1, 0)])  4.7 us
    pallas_call x1, Pallas kernels, shards(): call(functools.partial(rank_kernel, tiles, n_row, n_col), (shape((tiles,...  2.92 us
  transfers between devices with their start and end apart: 6, of which 2 were waited for; matrix products, arithmetic and copies ran while one was open for 2% of the time, Pallas kernels for 5%

profile of v2, /device:TPU:1, one launch (start us, length us, event | category | flops | bytes accessed | tf_op | source)
XLA Modules:
  0.0 82.1 jit_solution(745041675899151435)
XLA Ops:
  0.6 2.0 %stage.1 = (f32[1536,128]{1,0:T(8,128)}, f32[192,128]{1,0:T(8,128)}) custom-call(f32[3,3072]{1,0:T(4,128)} %pos.1, f32[3,3072]{1,0:T(4,128)} %nor.1, f32[1,3072]{1,0:T(1,128)} %bitcast.33, f32[1,3072]{1,0:T(1,128)} %bitcast.40, f32[8,3072]{1,0:T(8,128)} %basis.7), custom_call_target="tpu_custom_call" | custom-call | flops 1100000000 | bytes 65536 | tf_op jit(solution)/shard_map/stage/pallas_call | solution.py:376
  2.7 2.1 %collective-permute-start = (f32[192,128]{1,0:T(8,128)}, f32[192,128]{1,0:T(8,128)S(1)}, u32[]{:S(2)}, u32[]{:S(2)}) collective-permute-start(f32[192,128]{1,0:T(8,128)} %get-tuple-element.27), channel_id=1, source_target_pairs={{0,64},{64,0},{1,65},{65,1},{2,66},{66,2},{3,67},{67,3},{4,68},{68... | collective-permute-start | bytes 294920 | tf_op jit(solution)/shard_map/ppermute | solution.py:391
  4.8 0.9 %constant_dynamic-update-slice_fusion.1 = f32[384,128]{1,0:T(8,128)S(1)} fusion(f32[192,128]{1,0:T(8,128)} %get-tuple-element.27), kind=kLoop, calls=%fused_computation.1 | loop fusion | bytes 196608
  5.7 0.6 pad_add_fusion.place
  6.3 0.7 collective-permute-done
  7.0 1.6 %collective-permute-start.1 = (f32[384,128]{1,0:T(8,128)S(1)}, f32[384,128]{1,0:T(8,128)S(1)}, u32[]{:S(2)}, u32[]{:S(2)}) collective-permute-start(f32[384,128]{1,0:T(8,128)S(1)} %constant_dynamic-update-slice_fusion.refs_0_), channel_id=1, source_target_pairs={{0,16},{16,32},{32,48},{48,0},{1,17},{17,33},{33,49},{49,1},{2,18}... | collective-permute-start | bytes 589832 | tf_op jit(solution)/shard_map/ppermute | solution.py:411
  8.6 2.6 %collective-permute-start.2 = (f32[384,128]{1,0:T(8,128)S(1)}, f32[384,128]{1,0:T(8,128)S(1)}, u32[]{:S(2)}, u32[]{:S(2)}) collective-permute-start(f32[384,128]{1,0:T(8,128)S(1)} %constant_dynamic-update-slice_fusion.refs_0_), channel_id=1, source_target_pairs={{0,32},{16,48},{32,0},{48,16},{1,33},{17,49},{33,1},{49,17},{2,34}... | collective-permute-start | bytes 589832 | tf_op jit(solution)/shard_map/ppermute | solution.py:411
  11.3 1.1 %collective-permute-start.3 = (f32[384,128]{1,0:T(8,128)S(1)}, f32[384,128]{1,0:T(8,128)S(1)}, u32[]{:S(2)}, u32[]{:S(2)}) collective-permute-start(f32[384,128]{1,0:T(8,128)S(1)} %constant_dynamic-update-slice_fusion.refs_0_), channel_id=1, source_target_pairs={{0,48},{16,0},{32,16},{48,32},{1,49},{17,1},{33,17},{49,33},{2,50}... | collective-permute-start | bytes 589832 | tf_op jit(solution)/shard_map/ppermute | solution.py:411
  12.3 7.5 %all-to-all-start = ((f32[8,1,24576]{2,1,0:T(1,128)}), f32[8,1,24576]{2,1,0:T(1,128)S(1)}, u32[]{:S(2)}, u32[]{:S(2)}) async-start(f32[8,1,24576]{2,1,0:T(1,128)} %bitcast.39), calls=%async_computation | async-start | bytes 1572864 | tf_op jit(solution)/shard_map/all_to_all | solution.py:414
  19.8 2.9 %rank.1 = (s32[24,128]{1,0:T(8,128)}, f32[128,128]{1,0:T(8,128)}, f32[1,128]{1,0:T(1,128)}, s32[4,128]{1,0:T(4,128)}, s32[4,128]{1,0:T(4,128)}) custom-call(s32[3]{0:T(128)} %pad_add_fusion.place, s32[24,128]{1,0:T(8,128)} %bitcast.31, s32[24,128]{1,0:T(8,128)} %bitcast.41, f32[8,3072]{1,0:T(8,128)} %basis.7, s32[4,128]{1,0:T(4,128)} %bitcast.42, ...), custom_call_target="tpu_custom_call" | custom-call | flops 22000001024 | bytes 65536 | tf_op jit(solution)/shard_map/rank/pallas_call | solution.py:396
  22.7 0.0 copy-start
  22.7 0.0 copy-start.6
  22.7 0.0 copy-start.7
  22.7 0.0 collective-permute-done.1.refs_1_
  22.8 0.0 collective-permute-done.2.refs_2_
  22.8 0.0 collective-permute-done.3.refs_3_
  22.8 6.9 %all-to-all-done = f32[8,1,24576]{2,1,0:T(1,128)S(1)} async-done(((f32[8,1,24576]{2,1,0:T(1,128)}), f32[8,1,24576]{2,1,0:T(1,128)S(1)}, u32[]{:S(2)}, u32[]{:S(2)}) %all-to-all-start) | async-done | bytes 786464 | tf_op jit(solution)/shard_map/all_to_all | solution.py:414
  29.7 4.7 %collective-permute-start.4 = (f32[1536,128]{1,0:T(8,128)S(1)}, f32[1536,128]{1,0:T(8,128)S(1)}, u32[]{:S(2)}, u32[]{:S(2)}) collective-permute-start(f32[1536,128]{1,0:T(8,128)S(1)} %bitcast.25), channel_id=1, source_target_pairs={{0,1},{1,0},{2,3},{3,2},{4,5},{5,4},{6,7},{7,6},{8,9},{9,8},{10,11... | collective-permute-start | bytes 2359304 | tf_op jit(solution)/shard_map/ppermute | solution.py:418
  35.1 1.5 %receivers.1.wtab = bf16[192,64,384]{2,1,0:T(8,128)(2,1)S(1)} custom-call(f32[384,128]{1,0:T(8,128)S(1)} %constant_dynamic-update-slice_fusion.refs_0_, f32[384,128]{1,0:T(8,128)S(1)} %collective-permute-done.1.refs_1_, f32[384,128]{1,0:T(8,128)S(1)} %collective-permute-done.2.refs_2_, f32[384,128]{1,0:T(8,128)S(1)} %collective-permute-done.3.refs_3_), custom_call_target="tpu_custom_call" | custom-call | flops 4400000000 | bytes 65536 | tf_op jit(solution)/shard_map/receivers/pallas_call | solution.py:419
  36.6 0.0 collective-permute-done.4.far
  36.6 0.0 copy-done
  36.6 0.0 copy-done.6
  36.6 0.0 copy-done.7
  36.6 0.0 copy-start.1
  36.6 0.0 copy-start.2
  36.6 0.0 copy-start.3
  36.7 0.0 copy-start.4
  36.7 0.0 copy-start.5
  36.7 0.0 copy-start.8
  36.7 0.0 copy-start.9
  36.7 0.0 copy-start.10
  36.7 10.9 %pairs.1 = f32[384,128]{1,0:T(8,128)S(1)} custom-call(s32[1]{0:T(128)} %bitcast.24.count, s32[512]{0:T(512)S(1)} %bitcast.37, s32[512]{0:T(512)S(1)} %bitcast.38, s32[3]{0:T(128)S(1)} %copy-done, f32[1536,128]{1,0:T(8,128)S(1)} %bitcast.26, f32[1536,128]{1,0:T(8,128)S(1)} %collective-permute-done.4.far, bf16[192,64,384]{2,1,0:T(8,128)(2,1)S(1)} %receivers.1.wtab), custom_call_target="tpu_custom_call" | custom-call | flops 22000001024 | bytes 65536 | tf_op jit(solution)/shard_map/pairs/pallas_call | solution.py:427
  47.6 15.6 %all_to_all.27 = f32[8,1,6144]{2,1,0:T(1,128)S(1)} all-to-all(f32[8,1,6144]{2,1,0:T(1,128)S(1)} %bitcast.27), channel_id=1, replica_groups=mesh['pair'=2,'ring'=4,'half'=8,'core'=2] {'pair','ring'}, dimensions={0} | all-to-all | bytes 393216 | tf_op jit(solution)/shard_map/all_to_all | solution.py:448
  63.2 0.0 copy-done.1
  63.2 0.0 copy-done.2
  63.2 0.0 copy-done.3
  63.2 0.0 copy-done.4
  63.2 0.0 copy-done.5
  63.3 0.0 copy-done.8
  63.3 0.0 copy-done.9
  63.3 0.0 copy-done.10
  63.3 1.1 %loads.1 = (f32[256,128]{1,0:T(8,128)S(1)}, f32[24,128]{1,0:T(8,128)S(1)}) custom-call(f32[384,128]{1,0:T(8,128)S(1)} %bitcast.28, f32[8,3072]{1,0:T(8,128)S(1)} %copy-done.1, f32[24,128]{1,0:T(8,128)S(1)} %bitcast.35, f32[24,128]{1,0:T(8,128)S(1)} %bitcast.36, f32[24,128]{1,0:T(8,128)S(1)} %bitcast.34, s32[24,128]{1,0:T(8,128)S(1)} %bitcast.32, ...), custom_call_target="tpu_custom_call" | custom-call | flops 1100000000 | bytes 65536 | tf_op jit(solution)/shard_map/loads/pallas_call | solution.py:449
  64.4 15.6 %all_to_all.28 = f32[128,1,256]{2,1,0:T(1,128)S(1)} all-to-all(f32[128,1,256]{2,1,0:T(1,128)S(1)} %bitcast.29), channel_id=1, replica_groups=mesh['pair'=2,'ring'=4,'half'=8,'core'=2] {'pair','ring','half','core'}, dimensions={0} | all-to-all | bytes 262144 | tf_op jit(solution)/shard_map/all_to_all | solution.py:465
  80.1 2.0 %finish.1 = (f32[24,128]{1,0:T(8,128)}, f32[1,9]{1,0:T(1,128)}, f32[16,128]{1,0:T(8,128)}) custom-call(f32[256,128]{1,0:T(8,128)S(1)} %bitcast.30, f32[8,3072]{1,0:T(8,128)S(1)} %copy-done.1, f32[24,128]{1,0:T(8,128)S(1)} %get-tuple-element.45.damped), custom_call_target="tpu_custom_call" | custom-call | flops 1100000000 | bytes 65536 | tf_op jit(solution)/shard_map/finish/pallas_call | solution.py:466
  (1 shorter events, 0.0 us)
Async XLA Ops:
  2.7 4.3 %collective-permute-start = (f32[192,128]{1,0:T(8,128)}, f32[192,128]{1,0:T(8,128)S(1)}, u32[]{:S(2)}, u32[]{:S(2)}) collective-permute-start(f32[192,128]{1,0:T(8,128)} %get-tuple-element.27), channel_id=1, source_target_pairs={{0,64},{64,0},{1,65},{65,1},{2,66},{66,2},{3,67},{67,3},{4,68},{68... | collective-permute-start | bytes 294920 | tf_op jit(solution)/shard_map/ppermute | solution.py:391
  7.0 15.7 %collective-permute-start.1 = (f32[384,128]{1,0:T(8,128)S(1)}, f32[384,128]{1,0:T(8,128)S(1)}, u32[]{:S(2)}, u32[]{:S(2)}) collective-permute-start(f32[384,128]{1,0:T(8,128)S(1)} %constant_dynamic-update-slice_fusion.refs_0_), channel_id=1, source_target_pairs={{0,16},{16,32},{32,48},{48,0},{1,17},{17,33},{33,49},{49,1},{2,18}... | collective-permute-start | bytes 589832 | tf_op jit(solution)/shard_map/ppermute | solution.py:411
  8.6 14.1 %collective-permute-start.2 = (f32[384,128]{1,0:T(8,128)S(1)}, f32[384,128]{1,0:T(8,128)S(1)}, u32[]{:S(2)}, u32[]{:S(2)}) collective-permute-start(f32[384,128]{1,0:T(8,128)S(1)} %constant_dynamic-update-slice_fusion.refs_0_), channel_id=1, source_target_pairs={{0,32},{16,48},{32,0},{48,16},{1,33},{17,49},{33,1},{49,17},{2,34}... | collective-permute-start | bytes 589832 | tf_op jit(solution)/shard_map/ppermute | solution.py:411
  11.3 11.5 %collective-permute-start.3 = (f32[384,128]{1,0:T(8,128)S(1)}, f32[384,128]{1,0:T(8,128)S(1)}, u32[]{:S(2)}, u32[]{:S(2)}) collective-permute-start(f32[384,128]{1,0:T(8,128)S(1)} %constant_dynamic-update-slice_fusion.refs_0_), channel_id=1, source_target_pairs={{0,48},{16,0},{32,16},{48,32},{1,49},{17,1},{33,17},{49,33},{2,50}... | collective-permute-start | bytes 589832 | tf_op jit(solution)/shard_map/ppermute | solution.py:411
  12.3 17.4 %all-to-all-start = ((f32[8,1,24576]{2,1,0:T(1,128)}), f32[8,1,24576]{2,1,0:T(1,128)S(1)}, u32[]{:S(2)}, u32[]{:S(2)}) async-start(f32[8,1,24576]{2,1,0:T(1,128)} %bitcast.39), calls=%async_computation | async-start | bytes 1572864 | tf_op jit(solution)/shard_map/all_to_all | solution.py:414
  22.7 13.9 %copy-start = (s32[3]{0:T(128)S(1)}, s32[3]{0:T(128)}, u32[]{:S(2)}) copy-start(s32[3]{0:T(128)} %pad_add_fusion.place) | copy-start | bytes 40
  22.7 13.9 %copy-start.6 = (s32[4,128]{1,0:T(4,128)S(1)}, s32[4,128]{1,0:T(4,128)}, u32[]{:S(2)}) copy-start(s32[4,128]{1,0:T(4,128)} %get-tuple-element.34) | copy-start | bytes 6148
  22.7 13.9 %copy-start.7 = (s32[4,128]{1,0:T(4,128)S(1)}, s32[4,128]{1,0:T(4,128)}, u32[]{:S(2)}) copy-start(s32[4,128]{1,0:T(4,128)} %get-tuple-element.35) | copy-start | bytes 6148
  29.7 6.9 %collective-permute-start.4 = (f32[1536,128]{1,0:T(8,128)S(1)}, f32[1536,128]{1,0:T(8,128)S(1)}, u32[]{:S(2)}, u32[]{:S(2)}) collective-permute-start(f32[1536,128]{1,0:T(8,128)S(1)} %bitcast.25), channel_id=1, source_target_pairs={{0,1},{1,0},{2,3},{3,2},{4,5},{5,4},{6,7},{7,6},{8,9},{9,8},{10,11... | collective-permute-start | bytes 2359304 | tf_op jit(solution)/shard_map/ppermute | solution.py:418
  36.6 26.6 %copy-start.1 = (f32[8,3072]{1,0:T(8,128)S(1)}, f32[8,3072]{1,0:T(8,128)}, u32[]{:S(2)}) copy-start(f32[8,3072]{1,0:T(8,128)} %basis.7) | copy-start | bytes 294916
  36.6 26.6 %copy-start.2 = (s32[3072,1]{0,1:T(1,128)S(1)}, s32[3072,1]{0,1:T(1,128)}, u32[]{:S(2)}) copy-start(s32[3072,1]{0,1:T(1,128)} %param.22) | copy-start | bytes 36868
  36.6 26.6 %copy-start.3 = (f32[3072]{0:T(1024)S(1)}, f32[3072]{0:T(1024)}, u32[]{:S(2)}) copy-start(f32[3072]{0:T(1024)} %param.14) | copy-start | bytes 36868
  36.7 26.6 %copy-start.4 = (f32[3072]{0:T(1024)S(1)}, f32[3072]{0:T(1024)}, u32[]{:S(2)}) copy-start(f32[3072]{0:T(1024)} %param.15) | copy-start | bytes 36868
  36.7 26.6 %copy-start.5 = (f32[3072]{0:T(1024)S(1)}, f32[3072]{0:T(1024)}, u32[]{:S(2)}) copy-start(f32[3072]{0:T(1024)} %param.16) | copy-start | bytes 36868
  36.7 26.6 %copy-start.8 = (f32[128,128]{1,0:T(8,128)S(1)}, f32[128,128]{1,0:T(8,128)}, u32[]{:S(2)}) copy-start(f32[128,128]{1,0:T(8,128)} %get-tuple-element.42.slots) | copy-start | bytes 196612
  36.7 26.6 %copy-start.9 = (s32[24,128]{1,0:T(8,128)S(1)}, s32[24,128]{1,0:T(8,128)}, u32[]{:S(2)}) copy-start(s32[24,128]{1,0:T(8,128)} %get-tuple-element.41.rank) | copy-start | bytes 36868
  36.7 26.6 %copy-start.10 = (f32[1,128]{1,0:T(1,128)S(1)}, f32[1,128]{1,0:T(1,128)}, u32[]{:S(2)}) copy-start(f32[1,128]{1,0:T(1,128)} %get-tuple-element.43.gram) | copy-start | bytes 1540

commit v3 on v2

--- a/solution.py
+++ b/solution.py
@@ -43,39 +43,46 @@
     )
 
 
-def stage_kernel(tiles, copies, pos, nor, area, rad, basis, emit, recv, pos_v, nor_v, area_v, rad_v, last_v, sems):
+def fetch(sources, targets, sems):
     moves = [
         pltpu.make_async_copy(source, target, sems.at[k])
-        for k, (source, target) in enumerate(
-            (
-                (pos, pos_v),
-                (nor, nor_v),
-                (area, area_v),
-                (rad, rad_v),
-                (basis, last_v),
-            )
-        )
+        for k, (source, target) in enumerate(zip(sources, targets))
     ]
     for move in moves:
         move.start()
     for move in moves:
         move.wait()
+
+
+def emit_kernel(tiles, copies, pos, nor, area, rad, basis, emit, pos_v, nor_v, area_v, rad_v, basis_v, sems):
+    fetch((pos, nor, area, rad, basis), (pos_v, nor_v, area_v, rad_v, basis_v), sems)
     x = pos_v[...]
     n = nor_v[...]
     a = area_v[...]
     b = rad_v[...]
     m = (a * b * (1.0 / math.pi)) * n
-    product = n * x
     square = x * x
     square = square[0:1] + square[1:2] + square[2:3]
-    along = product[0:1] + product[1:2] + product[2:3]
-    emit_rows = jnp.concatenate([x, m, square + a, last_v[7:8, :] / b], 0)
-    recv_rows = jnp.concatenate([x, n, -along, square], 0)
+    emit_rows = jnp.concatenate([x, m, square + a, basis_v[7:8, :] / b], 0)
     for k in range(tiles):
         block = emit_rows[:, k * LANES : (k + 1) * LANES]
         for c in range(copies):
             emit[(c * tiles + k) * 8 : (c * tiles + k + 1) * 8, :] = block
-        recv[k * 8 : (k + 1) * 8, :] = recv_rows[:, k * LANES : (k + 1) * LANES]
+
+
+def join_kernel(tiles, own_pos, own_nor, pos, nor, both):
+    base = 0
+    for x_ref, n_ref in ((own_pos, own_nor), (pos, nor)):
+        x = x_ref[...]
+        n = n_ref[...]
+        product = n * x
+        square = x * x
+        square = square[0:1] + square[1:2] + square[2:3]
+        along = product[0:1] + product[1:2] + product[2:3]
+        rows = jnp.concatenate([x, n, -along, square], 0)
+        for k in range(tiles):
+            both[base + k * 8 : base + (k + 1) * 8, :] = rows[:, k * LANES : (k + 1) * LANES]
+        base += tiles * 8
 
 
 def rank_kernel(tiles, n_row, n_col, place, owner, elem, basis, recv_list, emit_list, rank, slots, gram, recv_at, emit_at):
@@ -211,20 +218,38 @@
     my_pair, my_ring = place[0], place[1]
     ring = n_row // 2
 
-    def pair(at):
-        r = recv_list[at]
-        e = emit_list[at]
-        g = lax.dot_general(etab[e], wtab[r], TN, preferred_element_type=F32)
+    empty = jnp.zeros((64, 3 * LANES), BF16)
+
+    def view(g, e):
         facing = jnp.maximum(g[:, :LANES], 0.0)
         away = jnp.maximum(g[:, LANES : 2 * LANES], 0.0)
         spread = g[:, 2 * LANES :]
         first = facing * away / (spread * spread)
         lane = jnp.full((LANES, LANES), e & (LANES - 1), jnp.int32)
         factor = jnp.take_along_axis(ratio[e >> 7], lane, axis=1, mode="promise_in_bounds")
-        return r, fold(first), fold(first * factor)
+        return fold(first), fold(first * factor)
+
+    def two(at):
+        r = recv_list[at], recv_list[at + 1]
+        e = emit_list[at], emit_list[at + 1]
+        weights = jnp.concatenate(
+            [
+                jnp.concatenate([wtab[r[0]], empty], 0),
+                jnp.concatenate([empty, wtab[r[1]]], 0),
+            ],
+            1,
+        )
+        g = lax.dot_general(
+            jnp.concatenate([etab[e[0]], etab[e[1]]], 0), weights, TN, preferred_element_type=F32
+        )
+        return [
+            (r[k],) + view(g[:, 3 * k * LANES : 3 * (k + 1) * LANES], e[k]) for k in range(2)
+        ]
 
     def step(i, _):
-        found = [pair(i * unroll + k) for k in range(unroll)]
+        found = []
+        for k in range(0, unroll, 2):
+            found += two(i * unroll + k)
         for k, (r, first, second) in enumerate(found):
             keep = jnp.where(i * unroll + k < live, 1.0, 0.0)
             at = pl.multiple_of(r * 16, 16)
@@ -373,9 +398,12 @@
     def rows(array):
         return array.reshape(-1, LANES)
 
-    emit, recv = call(
-        functools.partial(stage_kernel, tiles, half),
-        (shape((half * 8 * tiles, LANES), F32), shape((8 * tiles, LANES), F32)),
+    hbm = pl.BlockSpec(memory_space=pl.ANY)
+    swap = [(0, 1), (1, 0)]
+    swapped = [lax.ppermute(array, "pair", swap) for array in (positions, normals)]
+    emit = call(
+        functools.partial(emit_kernel, tiles, half),
+        shape((half * 8 * tiles, LANES), F32),
         scratch=[
             pltpu.VMEM((3, patches), F32),
             pltpu.VMEM((3, patches), F32),
@@ -384,13 +412,18 @@
             pltpu.VMEM((8, patches), F32),
             pltpu.SemaphoreType.DMA((5,)),
         ],
-        in_specs=[pl.BlockSpec(memory_space=pl.ANY)] * 5,
-        name="stage",
+        in_specs=[hbm] * 5,
+        name="emit",
+        micros=4,
         limit=60 * 2**20,
     )(positions, normals, patch_extents[None], radiosity[None], basis)
-    swapped = lax.ppermute(recv, "pair", [(0, 1), (1, 0)])
-    emit, swapped = lax.optimization_barrier((emit, swapped))
-    both = jnp.concatenate([recv, swapped], 0)
+    both = call(
+        functools.partial(join_kernel, tiles),
+        shape((16 * tiles, LANES), F32),
+        in_specs=[VMEM] * 4,
+        name="join",
+        micros=3,
+    )(positions, normals, *swapped)
     owner_rows, both_again = lax.optimization_barrier((rows(owner), both))
     lists = rows(recv_blocks), rows(emit_blocks)
     rank, slots, gram, recv_at, emit_at = call(
@@ -404,7 +437,7 @@
         ),
         in_specs=[SMEM] + [VMEM] * 5,
         name="rank",
-        micros=20,
+        micros=3,
         limit=60 * 2**20,
     )(place, owner_rows, rows(local_elem), basis, *lists)
     received = [both_again] + [
@@ -423,7 +456,7 @@
         name="receivers",
         micros=4,
     )(*received)
-    unroll = 32
+    unroll = 64
     part = call(
         functools.partial(pair_kernel, tiles, n_row, n_col, unroll),
         shape((n_row * 2 * tiles, LANES), F32),

time: 82.6 us -> 78.1 us (0.946)
  waiting for transfers between devices: 7.64 us -> 3.63 us
  blocking collectives: 31.2 us -> 34.5 us
  starting transfers between devices: 19.6 us -> 17.4 us
  Pallas kernels: 20.5 us -> 19.5 us
  local copies, waits for them, and re-layouts: 1 us -> 0.07 us
    all_to_all x1, waiting for transfers between devices: 6.92 us -> 0.01 us  [shards(): lax.all_to_all(emit.reshape(half, -1), 'half', 0, 0, tiled=True)]
    all_to_all x1, blocking collectives: 15.6 us -> 21.3 us  [shards(): lax.all_to_all(message.reshape(devices, -1), AXES, 0, 0, tiled=True)]
    ppermute x3, waiting for transfers between devices: 0.01 us -> 3.62 us  [shards(): lax.ppermute(both, 'ring', [(i, (i + k) % ring) for i in range(ring)])]
    all_to_all x1, blocking collectives: 15.6 us -> 13.2 us  [shards(): part = lax.all_to_all(part.reshape(n_row, -1), ROW, 0, 0, tiled=True)]
    ppermute x1, starting transfers between devices: 4.7 us -> 2.44 us  [shards(): far = lax.ppermute(near, 'core', [(0, 1), (1, 0)])]
    pallas_call x1, Pallas kernels: 10.9 us -> 9.81 us  [shards(): call(functools.partial(pair_kernel, tiles, n_row, n_col, unroll), shape((...]
    unnamed x23 -> x26, local copies, waits for them, and re-layouts: 0.99 us -> 0.07 us
    ppermute x1 -> x2, starting transfers between devices: 2.12 us -> 2.21 us  [shards(): lax.ppermute(array, 'pair', swap)]
  transfers between devices with their start and end apart: 6 -> 7, of which waited for: 2 -> 1; matrix products, arithmetic and copies ran while one was open for 2% -> 1% of each run, Pallas kernels for 5% -> 8%
where the time goes in v3:
time: 78.1 us; the launch traced here: 77.2 us
  blocking collectives  34.5 us (44%)
  Pallas kernels  19.5 us (25%)
  starting transfers between devices  17.4 us (22%)
  waiting for transfers between devices  3.63 us (5%)
  between operations  1.51 us (2%)
    all_to_all x1, blocking collectives, shards(): lax.all_to_all(message.reshape(devices, -1), AXES, 0, 0, tiled=True)  21.3 us
    all_to_all x1, blocking collectives, shards(): part = lax.all_to_all(part.reshape(n_row, -1), ROW, 0, 0, tiled=True)  13.2 us
    pallas_call x1, Pallas kernels, shards(): call(functools.partial(pair_kernel, tiles, n_row, n_col, unroll), shape((...  9.81 us
    all_to_all x1, starting transfers between devices, shards(): lax.all_to_all(emit.reshape(half, -1), 'half', 0, 0, tiled=True)  7.67 us
    ppermute x3, starting transfers between devices, shards(): lax.ppermute(both, 'ring', [(i, (i + k) % ring) for i in range(ring)])  5.05 us
    ppermute x3, waiting for transfers between devices, shards(): lax.ppermute(both, 'ring', [(i, (i + k) % ring) for i in range(ring)])  3.62 us
    pallas_call x1, Pallas kernels, shards(): call(functools.partial(rank_kernel, tiles, n_row, n_col), (shape((tiles,...  2.91 us
    ppermute x1, starting transfers between devices, shards(): far = lax.ppermute(near, 'core', [(0, 1), (1, 0)])  2.44 us
  transfers between devices with their start and end apart: 7, of which 1 were waited for; matrix products, arithmetic and copies ran while one was open for 1% of the time, Pallas kernels for 8%

profile of v3, /device:TPU:1, one launch (start us, length us, event | category | flops | bytes accessed | tf_op | source)
XLA Modules:
  0.0 77.2 jit_solution(13117752716303160836)
XLA Ops:
  0.6 0.0 copy-start.2
  0.6 0.0 copy-start.3
  0.7 2.1 %collective-permute-start = (f32[3,3072]{1,0:T(4,128)}, f32[3,3072]{1,0:T(4,128)S(1)}, u32[]{:S(2)}, u32[]{:S(2)}) collective-permute-start(f32[3,3072]{1,0:T(4,128)} %own_pos.1), channel_id=1, source_target_pairs={{0,64},{64,0},{1,65},{65,1},{2,66},{66,2},{3,67},{67,3},{4,68},{68... | collective-permute-start | bytes 110600 | tf_op jit(solution)/shard_map/ppermute | solution.py:403
  2.8 0.1 collective-permute-start.1
  2.9 2.0 %emit.1 = f32[1536,128]{1,0:T(8,128)} custom-call(f32[3,3072]{1,0:T(4,128)} %own_pos.1, f32[3,3072]{1,0:T(4,128)} %own_nor.1, f32[1,3072]{1,0:T(1,128)} %bitcast.33, f32[1,3072]{1,0:T(1,128)} %bitcast.40, f32[8,3072]{1,0:T(8,128)} %basis.7), custom_call_target="tpu_custom_call" | custom-call | flops 4400000000 | bytes 65536 | tf_op jit(solution)/shard_map/emit/pallas_call | solution.py:404
  4.8 7.7 %all-to-all-start = ((f32[8,1,24576]{2,1,0:T(1,128)}), f32[8,1,24576]{2,1,0:T(1,128)S(1)}, u32[]{:S(2)}, u32[]{:S(2)}) async-start(f32[8,1,24576]{2,1,0:T(1,128)} %bitcast.39), calls=%async_computation | async-start | bytes 1572864 | tf_op jit(solution)/shard_map/all_to_all | solution.py:447
  12.5 0.7 pad_add_fusion.place
  13.2 0.0 collective-permute-done.pos
  13.2 0.0 collective-permute-done.1.nor
  13.2 0.0 copy-done.2
  13.2 0.0 copy-done.3
  13.2 0.1 join.1.refs_0_
  13.3 1.4 %collective-permute-start.2 = (f32[384,128]{1,0:T(8,128)S(1)}, f32[384,128]{1,0:T(8,128)S(1)}, u32[]{:S(2)}, u32[]{:S(2)}) collective-permute-start(f32[384,128]{1,0:T(8,128)S(1)} %join.1.refs_0_), channel_id=1, source_target_pairs={{0,16},{16,32},{32,48},{48,0},{1,17},{17,33},{33,49},{49,1},{2,18}... | collective-permute-start | bytes 589832 | tf_op jit(solution)/shard_map/ppermute | solution.py:444
  14.7 2.6 %collective-permute-start.3 = (f32[384,128]{1,0:T(8,128)S(1)}, f32[384,128]{1,0:T(8,128)S(1)}, u32[]{:S(2)}, u32[]{:S(2)}) collective-permute-start(f32[384,128]{1,0:T(8,128)S(1)} %join.1.refs_0_), channel_id=1, source_target_pairs={{0,32},{16,48},{32,0},{48,16},{1,33},{17,49},{33,1},{49,17},{2,34}... | collective-permute-start | bytes 589832 | tf_op jit(solution)/shard_map/ppermute | solution.py:444
  17.3 1.1 %collective-permute-start.4 = (f32[384,128]{1,0:T(8,128)S(1)}, f32[384,128]{1,0:T(8,128)S(1)}, u32[]{:S(2)}, u32[]{:S(2)}) collective-permute-start(f32[384,128]{1,0:T(8,128)S(1)} %join.1.refs_0_), channel_id=1, source_target_pairs={{0,48},{16,0},{32,16},{48,32},{1,49},{17,1},{33,17},{49,33},{2,50}... | collective-permute-start | bytes 589832 | tf_op jit(solution)/shard_map/ppermute | solution.py:444
  18.3 2.9 %rank.1 = (s32[24,128]{1,0:T(8,128)}, f32[128,128]{1,0:T(8,128)}, f32[1,128]{1,0:T(1,128)}, s32[4,128]{1,0:T(4,128)}, s32[4,128]{1,0:T(4,128)}) custom-call(s32[3]{0:T(128)} %pad_add_fusion.place, s32[24,128]{1,0:T(8,128)} %bitcast.31, s32[24,128]{1,0:T(8,128)} %bitcast.41, f32[8,3072]{1,0:T(8,128)} %basis.7, s32[4,128]{1,0:T(4,128)} %bitcast.42, ...), custom_call_target="tpu_custom_call" | custom-call | flops 3300000000 | bytes 65536 | tf_op jit(solution)/shard_map/rank/pallas_call | solution.py:429
  21.3 0.0 copy-start
  21.3 0.0 copy-start.8
  21.3 0.0 copy-start.9
  21.3 0.0 collective-permute-done.2.refs_1_
  21.3 3.6 %collective-permute-done.3.refs_2_ = f32[384,128]{1,0:T(8,128)S(1)} collective-permute-done((f32[384,128]{1,0:T(8,128)S(1)}, f32[384,128]{1,0:T(8,128)S(1)}, u32[]{:S(2)}, u32[]{:S(2)}) %collective-permute-start.3) | collective-permute-done | bytes 196640 | tf_op jit(solution)/shard_map/ppermute | solution.py:444
  24.9 0.0 collective-permute-done.4.refs_3_
  24.9 0.0 all-to-all-done
  24.9 2.4 %collective-permute-start.5 = (f32[1536,128]{1,0:T(8,128)S(1)}, f32[1536,128]{1,0:T(8,128)S(1)}, u32[]{:S(2)}, u32[]{:S(2)}) collective-permute-start(f32[1536,128]{1,0:T(8,128)S(1)} %bitcast.25), channel_id=1, source_target_pairs={{0,1},{1,0},{2,3},{3,2},{4,5},{5,4},{6,7},{7,6},{8,9},{9,8},{10,11... | collective-permute-start | bytes 2359304 | tf_op jit(solution)/shard_map/ppermute | solution.py:451
  28.0 1.5 %receivers.1.wtab = bf16[192,64,384]{2,1,0:T(8,128)(2,1)S(1)} custom-call(f32[384,128]{1,0:T(8,128)S(1)} %join.1.refs_0_, f32[384,128]{1,0:T(8,128)S(1)} %collective-permute-done.2.refs_1_, f32[384,128]{1,0:T(8,128)S(1)} %collective-permute-done.3.refs_2_, f32[384,128]{1,0:T(8,128)S(1)} %collective-permute-done.4.refs_3_), custom_call_target="tpu_custom_call" | custom-call | flops 4400000000 | bytes 65536 | tf_op jit(solution)/shard_map/receivers/pallas_call | solution.py:452
  29.5 0.0 collective-permute-done.5.far
  29.5 0.0 copy-done
  29.5 0.0 copy-done.8
  29.5 0.0 copy-done.9
  29.6 0.0 copy-start.1
  29.6 0.0 copy-start.4
  29.6 0.0 copy-start.5
  29.6 0.0 copy-start.6
  29.6 0.0 copy-start.7
  29.6 0.0 copy-start.10
  29.6 0.0 copy-start.11
  29.6 0.0 copy-start.12
  29.7 9.8 %pairs.1 = f32[384,128]{1,0:T(8,128)S(1)} custom-call(s32[1]{0:T(128)} %bitcast.24.count, s32[512]{0:T(512)S(1)} %bitcast.37, s32[512]{0:T(512)S(1)} %bitcast.38, s32[3]{0:T(128)S(1)} %copy-done, f32[1536,128]{1,0:T(8,128)S(1)} %bitcast.26, f32[1536,128]{1,0:T(8,128)S(1)} %collective-permute-done.5.far, bf16[192,64,384]{2,1,0:T(8,128)(2,1)S(1)} %receivers.1.wtab), custom_call_target="tpu_custom_call" | custom-call | flops 22000001024 | bytes 65536 | tf_op jit(solution)/shard_map/pairs/pallas_call | solution.py:460
  39.5 13.2 %all_to_all.27 = f32[8,1,6144]{2,1,0:T(1,128)S(1)} all-to-all(f32[8,1,6144]{2,1,0:T(1,128)S(1)} %bitcast.27), channel_id=1, replica_groups=mesh['pair'=2,'ring'=4,'half'=8,'core'=2] {'pair','ring'}, dimensions={0} | all-to-all | bytes 393216 | tf_op jit(solution)/shard_map/all_to_all | solution.py:481
  52.7 0.0 copy-done.1
  52.7 0.0 copy-done.4
  52.7 0.0 copy-done.5
  52.7 0.0 copy-done.6
  52.7 0.0 copy-done.7
  52.7 0.0 copy-done.10
  52.7 0.0 copy-done.11
  52.7 0.0 copy-done.12
  52.7 1.1 %loads.1 = (f32[256,128]{1,0:T(8,128)S(1)}, f32[24,128]{1,0:T(8,128)S(1)}) custom-call(f32[384,128]{1,0:T(8,128)S(1)} %bitcast.28, f32[8,3072]{1,0:T(8,128)S(1)} %copy-done.1, f32[24,128]{1,0:T(8,128)S(1)} %bitcast.35, f32[24,128]{1,0:T(8,128)S(1)} %bitcast.36, f32[24,128]{1,0:T(8,128)S(1)} %bitcast.34, s32[24,128]{1,0:T(8,128)S(1)} %bitcast.32, ...), custom_call_target="tpu_custom_call" | custom-call | flops 1100000000 | bytes 65536 | tf_op jit(solution)/shard_map/loads/pallas_call | solution.py:482
  53.9 21.3 %all_to_all.28 = f32[128,1,256]{2,1,0:T(1,128)S(1)} all-to-all(f32[128,1,256]{2,1,0:T(1,128)S(1)} %bitcast.29), channel_id=1, replica_groups=mesh['pair'=2,'ring'=4,'half'=8,'core'=2] {'pair','ring','half','core'}, dimensions={0} | all-to-all | bytes 262144 | tf_op jit(solution)/shard_map/all_to_all | solution.py:498
  75.2 2.0 %finish.1 = (f32[24,128]{1,0:T(8,128)}, f32[1,9]{1,0:T(1,128)}, f32[16,128]{1,0:T(8,128)}) custom-call(f32[256,128]{1,0:T(8,128)S(1)} %bitcast.30, f32[8,3072]{1,0:T(8,128)S(1)} %copy-done.1, f32[24,128]{1,0:T(8,128)S(1)} %get-tuple-element.37.damped), custom_call_target="tpu_custom_call" | custom-call | flops 1100000000 | bytes 65536 | tf_op jit(solution)/shard_map/finish/pallas_call | solution.py:499
Async XLA Ops:
  0.6 12.6 %copy-start.2 = (f32[3,3072]{1,0:T(4,128)S(1)}, f32[3,3072]{1,0:T(4,128)}, u32[]{:S(2)}) copy-start(f32[3,3072]{1,0:T(4,128)} %own_pos.1) | copy-start | bytes 110596
  0.6 12.5 %copy-start.3 = (f32[3,3072]{1,0:T(4,128)S(1)}, f32[3,3072]{1,0:T(4,128)}, u32[]{:S(2)}) copy-start(f32[3,3072]{1,0:T(4,128)} %own_nor.1) | copy-start | bytes 110596
  0.7 12.5 %collective-permute-start = (f32[3,3072]{1,0:T(4,128)}, f32[3,3072]{1,0:T(4,128)S(1)}, u32[]{:S(2)}, u32[]{:S(2)}) collective-permute-start(f32[3,3072]{1,0:T(4,128)} %own_pos.1), channel_id=1, source_target_pairs={{0,64},{64,0},{1,65},{65,1},{2,66},{66,2},{3,67},{67,3},{4,68},{68... | collective-permute-start | bytes 110600 | tf_op jit(solution)/shard_map/ppermute | solution.py:403
  2.8 10.4 %collective-permute-start.1 = (f32[3,3072]{1,0:T(4,128)}, f32[3,3072]{1,0:T(4,128)S(1)}, u32[]{:S(2)}, u32[]{:S(2)}) collective-permute-start(f32[3,3072]{1,0:T(4,128)} %own_nor.1), channel_id=1, source_target_pairs={{0,64},{64,0},{1,65},{65,1},{2,66},{66,2},{3,67},{67,3},{4,68},{68... | collective-permute-start | bytes 110600 | tf_op jit(solution)/shard_map/ppermute | solution.py:403
  4.8 20.1 %all-to-all-start = ((f32[8,1,24576]{2,1,0:T(1,128)}), f32[8,1,24576]{2,1,0:T(1,128)S(1)}, u32[]{:S(2)}, u32[]{:S(2)}) async-start(f32[8,1,24576]{2,1,0:T(1,128)} %bitcast.39), calls=%async_computation | async-start | bytes 1572864 | tf_op jit(solution)/shard_map/all_to_all | solution.py:447
  13.3 8.0 %collective-permute-start.2 = (f32[384,128]{1,0:T(8,128)S(1)}, f32[384,128]{1,0:T(8,128)S(1)}, u32[]{:S(2)}, u32[]{:S(2)}) collective-permute-start(f32[384,128]{1,0:T(8,128)S(1)} %join.1.refs_0_), channel_id=1, source_target_pairs={{0,16},{16,32},{32,48},{48,0},{1,17},{17,33},{33,49},{49,1},{2,18}... | collective-permute-start | bytes 589832 | tf_op jit(solution)/shard_map/ppermute | solution.py:444
  14.7 10.2 %collective-permute-start.3 = (f32[384,128]{1,0:T(8,128)S(1)}, f32[384,128]{1,0:T(8,128)S(1)}, u32[]{:S(2)}, u32[]{:S(2)}) collective-permute-start(f32[384,128]{1,0:T(8,128)S(1)} %join.1.refs_0_), channel_id=1, source_target_pairs={{0,32},{16,48},{32,0},{48,16},{1,33},{17,49},{33,1},{49,17},{2,34}... | collective-permute-start | bytes 589832 | tf_op jit(solution)/shard_map/ppermute | solution.py:444
  17.3 7.6 %collective-permute-start.4 = (f32[384,128]{1,0:T(8,128)S(1)}, f32[384,128]{1,0:T(8,128)S(1)}, u32[]{:S(2)}, u32[]{:S(2)}) collective-permute-start(f32[384,128]{1,0:T(8,128)S(1)} %join.1.refs_0_), channel_id=1, source_target_pairs={{0,48},{16,0},{32,16},{48,32},{1,49},{17,1},{33,17},{49,33},{2,50}... | collective-permute-start | bytes 589832 | tf_op jit(solution)/shard_map/ppermute | solution.py:444
  21.3 8.3 %copy-start = (s32[3]{0:T(128)S(1)}, s32[3]{0:T(128)}, u32[]{:S(2)}) copy-start(s32[3]{0:T(128)} %pad_add_fusion.place) | copy-start | bytes 40
  21.3 8.3 %copy-start.8 = (s32[4,128]{1,0:T(4,128)S(1)}, s32[4,128]{1,0:T(4,128)}, u32[]{:S(2)}) copy-start(s32[4,128]{1,0:T(4,128)} %get-tuple-element.26) | copy-start | bytes 6148
  21.3 8.3 %copy-start.9 = (s32[4,128]{1,0:T(4,128)S(1)}, s32[4,128]{1,0:T(4,128)}, u32[]{:S(2)}) copy-start(s32[4,128]{1,0:T(4,128)} %get-tuple-element.27) | copy-start | bytes 6148
  24.9 4.6 %collective-permute-start.5 = (f32[1536,128]{1,0:T(8,128)S(1)}, f32[1536,128]{1,0:T(8,128)S(1)}, u32[]{:S(2)}, u32[]{:S(2)}) collective-permute-start(f32[1536,128]{1,0:T(8,128)S(1)} %bitcast.25), channel_id=1, source_target_pairs={{0,1},{1,0},{2,3},{3,2},{4,5},{5,4},{6,7},{7,6},{8,9},{9,8},{10,11... | collective-permute-start | bytes 2359304 | tf_op jit(solution)/shard_map/ppermute | solution.py:451
  29.6 23.1 %copy-start.1 = (f32[8,3072]{1,0:T(8,128)S(1)}, f32[8,3072]{1,0:T(8,128)}, u32[]{:S(2)}) copy-start(f32[8,3072]{1,0:T(8,128)} %basis.7) | copy-start | bytes 294916
  29.6 23.1 %copy-start.4 = (s32[3072,1]{0,1:T(1,128)S(1)}, s32[3072,1]{0,1:T(1,128)}, u32[]{:S(2)}) copy-start(s32[3072,1]{0,1:T(1,128)} %param.22) | copy-start | bytes 36868
  29.6 23.1 %copy-start.5 = (f32[3072]{0:T(1024)S(1)}, f32[3072]{0:T(1024)}, u32[]{:S(2)}) copy-start(f32[3072]{0:T(1024)} %param.14) | copy-start | bytes 36868
  29.6 23.1 %copy-start.6 = (f32[3072]{0:T(1024)S(1)}, f32[3072]{0:T(1024)}, u32[]{:S(2)}) copy-start(f32[3072]{0:T(1024)} %param.15) | copy-start | bytes 36868
  29.6 23.1 %copy-start.7 = (f32[3072]{0:T(1024)S(1)}, f32[3072]{0:T(1024)}, u32[]{:S(2)}) copy-start(f32[3072]{0:T(1024)} %param.16) | copy-start | bytes 36868
  29.6 23.1 %copy-start.10 = (f32[128,128]{1,0:T(8,128)S(1)}, f32[128,128]{1,0:T(8,128)}, u32[]{:S(2)}) copy-start(f32[128,128]{1,0:T(8,128)} %get-tuple-element.34.slots) | copy-start | bytes 196612
  29.6 23.1 %copy-start.11 = (s32[24,128]{1,0:T(8,128)S(1)}, s32[24,128]{1,0:T(8,128)}, u32[]{:S(2)}) copy-start(s32[24,128]{1,0:T(8,128)} %get-tuple-element.33.rank) | copy-start | bytes 36868
  29.6 23.1 %copy-start.12 = (f32[1,128]{1,0:T(1,128)S(1)}, f32[1,128]{1,0:T(1,128)}, u32[]{:S(2)}) copy-start(f32[1,128]{1,0:T(1,128)} %get-tuple-element.35.gram) | copy-start | bytes 1540

commit v4 on v3

--- a/solution.py
+++ b/solution.py
@@ -71,22 +71,17 @@
 
 
 def join_kernel(tiles, own_pos, own_nor, pos, nor, both):
-    base = 0
-    for x_ref, n_ref in ((own_pos, own_nor), (pos, nor)):
-        x = x_ref[...]
-        n = n_ref[...]
-        product = n * x
-        square = x * x
-        square = square[0:1] + square[1:2] + square[2:3]
-        along = product[0:1] + product[1:2] + product[2:3]
-        rows = jnp.concatenate([x, n, -along, square], 0)
-        for k in range(tiles):
-            both[base + k * 8 : base + (k + 1) * 8, :] = rows[:, k * LANES : (k + 1) * LANES]
-        base += tiles * 8
-
-
-def rank_kernel(tiles, n_row, n_col, place, owner, elem, basis, recv_list, emit_list, rank, slots, gram, recv_at, emit_at):
-    my_pair, my_ring, my_core = place[0], place[1], place[2]
+    blocks = 2 * tiles
+    for side, arrays in enumerate(((own_pos, own_nor), (pos, nor))):
+        for v, array in enumerate(arrays):
+            for k in range(tiles):
+                both[pl.ds(3 * v * blocks + side * tiles + k, 3, stride=blocks), :] = array[
+                    :, k * LANES : (k + 1) * LANES
+                ]
+
+
+def rank_kernel(tiles, n_row, n_col, owner, elem, basis, recv_list, emit_list, rank, slots, gram, recv_at, emit_at):
+    my_pair, my_ring, my_core = (lax.axis_index(a) for a in ("pair", "ring", "core"))
     ring = n_row // 2
     step_of = -(-65536 // tiles)
     r = recv_list[...]
@@ -134,15 +129,22 @@
 
 
 def receiver_kernel(*refs):
-    wtab = refs[-1]
+    wtab, consts_of = refs[-2:]
     row = lax.broadcasted_iota(jnp.int32, (8, LANES), 0)
     zero = jnp.zeros((8, LANES), F32)
     base = 0
-    for recv in refs[:-1]:
-        blocks = recv.shape[0] // 8
+    for recv in refs[:-2]:
+        blocks = recv.shape[0] // 6
+        x = [recv[f * blocks : (f + 1) * blocks, :] for f in range(6)]
+        consts_of[0] = -(x[0] * x[3] + x[1] * x[4] + x[2] * x[5])
+        consts_of[1] = x[0] * x[0] + x[1] * x[1] + x[2] * x[2]
 
         def body(k, _):
-            block = recv[pl.ds(pl.multiple_of(k * 8, 8), 8), :]
+            block = jnp.concatenate(
+                [recv[pl.ds(k, 6, stride=blocks), :]]
+                + [consts_of[f, pl.ds(k, 1), :] for f in range(2)],
+                0,
+            )
             parts = split3(block)
             facing, away, spread = [], [], []
             for p, part in enumerate(parts):
@@ -171,7 +173,7 @@
         base += blocks
 
 
-def pair_kernel(tiles, n_row, n_col, unroll, count, recv_list, emit_list, place, near, far, wtab, out, etab, along, ratio, acc):
+def pair_kernel(tiles, n_row, n_col, unroll, count, recv_list, emit_list, near, far, wtab, out, etab, along, ratio, acc):
     row = lax.broadcasted_iota(jnp.int32, (8, LANES), 0)
     ones3 = jnp.where(row < 3, 1.0, 0.0)
     half = n_col // 2
@@ -215,7 +217,7 @@
             total = total + full[8 * k : 8 * k + 8]
         return total
 
-    my_pair, my_ring = place[0], place[1]
+    my_pair, my_ring = lax.axis_index("pair"), lax.axis_index("ring")
     ring = n_row // 2
 
     empty = jnp.zeros((64, 3 * LANES), BF16)
@@ -282,12 +284,14 @@
     load = 20.0 * area[...] * jnp.sqrt(jnp.sqrt(power))
     parts = split3(load)
     found = jnp.zeros((LANES, LANES), F32)
-    for g in range(tiles):
-        hot = jnp.where(owner[g : g + 1, :] == sub, 1.0, 0.0).astype(BF16)
-        at = rank[g : g + 1, :] == sub
-        table = jnp.concatenate([jnp.where(at, v[g : g + 1, :], 0.0) for v in parts], 1)
+    for begin in range(0, tiles, 4):
+        hots, tables = [], []
+        for g in range(begin, begin + 4):
+            hots += [jnp.where(owner[g : g + 1, :] == sub, 1.0, 0.0).astype(BF16)] * 3
+            at = rank[g : g + 1, :] == sub
+            tables += [jnp.where(at, v[g : g + 1, :], 0.0).astype(BF16) for v in parts]
         found = found + lax.dot_general(
-            jnp.concatenate([hot] * 3, 1), table.astype(BF16), NT, preferred_element_type=F32
+            jnp.concatenate(hots, 1), jnp.concatenate(tables, 1), NT, preferred_element_type=F32
         )
     lanes = lax.broadcasted_iota(jnp.int32, (8, LANES), 1)
     subs = lax.broadcasted_iota(jnp.int32, (8, LANES), 0)
@@ -334,13 +338,14 @@
             line = line + 2.0 * gram[i, j] * left[j]
         square = square + line * left[i]
     length = jnp.sqrt(jnp.maximum(square, 0.0) * scale + 1e-6)
+    inverse = 1.0 / length
     subs = lax.broadcasted_iota(jnp.int32, (8, LANES), 0)
     weights = jnp.zeros((8, LANES), F32)
     for k in range(8):
         weights = jnp.where(subs == k, left[k], weights)
     for g in range(tiles):
         mixed = jnp.sum(basis[:, g * LANES : (g + 1) * LANES] * weights, axis=0, keepdims=True)
-        vector[g : g + 1, :] = (mixed - damped[g : g + 1, :]) / length
+        vector[g : g + 1, :] = (mixed - damped[g : g + 1, :]) * inverse
     lanes = lax.broadcasted_iota(jnp.int32, (1, LANES), 1)
     column = jnp.where(lanes == 8, length, 0.0)
     for k in range(8):
@@ -353,9 +358,9 @@
     sub = lax.broadcasted_iota(jnp.int32, (LANES, LANES), 0)
     sub16 = lax.broadcasted_iota(jnp.int32, (16, LANES), 0)
     total = jnp.zeros((48, LANES), F32)
-    for s in range(0, LANES, 2):
+    for s in range(0, LANES, 8):
         left_side, right_side = [], []
-        for u in (s, s + 1):
+        for u in range(s, s + 8):
             index = index_rows[u : u + 1, :]
             mask = (index >> 7) == sub16
             left_side.append(
@@ -392,7 +397,6 @@
     pairs_of, ring, half, cores = (lax.axis_size(a) for a in AXES)
     n_row, n_col = pairs_of * ring, half * cores
     devices = n_row * n_col
-    place = jnp.stack([lax.axis_index(a) for a in ("pair", "ring", "core")])
     shape = jax.ShapeDtypeStruct
 
     def rows(array):
@@ -417,9 +421,10 @@
         micros=4,
         limit=60 * 2**20,
     )(positions, normals, patch_extents[None], radiosity[None], basis)
+    emit, swapped = lax.optimization_barrier((emit, swapped))
     both = call(
         functools.partial(join_kernel, tiles),
-        shape((16 * tiles, LANES), F32),
+        shape((12 * tiles, LANES), F32),
         in_specs=[VMEM] * 4,
         name="join",
         micros=3,
@@ -435,11 +440,11 @@
             shape(lists[0].shape, jnp.int32),
             shape(lists[1].shape, jnp.int32),
         ),
-        in_specs=[SMEM] + [VMEM] * 5,
+        in_specs=[VMEM] * 5,
         name="rank",
         micros=3,
         limit=60 * 2**20,
-    )(place, owner_rows, rows(local_elem), basis, *lists)
+    )(owner_rows, rows(local_elem), basis, *lists)
     received = [both_again] + [
         lax.ppermute(both, "ring", [(i, (i + k) % ring) for i in range(ring)])
         for k in range(1, ring)
@@ -452,6 +457,7 @@
     wtab = call(
         receiver_kernel,
         shape((n_row * tiles, 64, 3 * LANES), BF16),
+        scratch=[pltpu.VMEM((2, 2 * tiles, LANES), F32)],
         in_specs=[VMEM] * len(received),
         name="receivers",
         micros=4,
@@ -466,14 +472,13 @@
             pltpu.VMEM((n_col * tiles // LANES, LANES, LANES), F32),
             pltpu.VMEM((n_row * tiles * 16, LANES), F32),
         ],
-        in_specs=[SMEM] * 4 + [VMEM] * 3,
+        in_specs=[SMEM] * 3 + [VMEM] * 3,
         name="pairs",
         micros=20,
     )(
         vis_count.reshape(-1),
         recv_at.reshape(-1),
         emit_at.reshape(-1),
-        place,
         near,
         far,
         wtab,

time: 78.1 us -> 76.3 us (0.977)
  blocking collectives: 34.5 us -> 30.1 us
  Pallas kernels: 19.5 us -> 21.3 us
  starting transfers between devices: 17.4 us -> 18.6 us
    all_to_all x1, blocking collectives: 21.3 us -> 14.9 us  [shards(): lax.all_to_all(message.reshape(devices, -1), AXES, 0, 0, tiled=True)]
    ppermute x3, waiting for transfers between devices: 3.62 us -> 1.55 us  [shards(): lax.ppermute(both, 'ring', [(i, (i + k) % ring) for i in range(ring)])]
    all_to_all x1, blocking collectives: 13.2 us -> 15.2 us  [shards(): part = lax.all_to_all(part.reshape(n_row, -1), ROW, 0, 0, tiled=True)]
    pallas_call x1, Pallas kernels: 9.81 us -> 11.7 us  [shards(): call(functools.partial(pair_kernel, tiles, n_row, n_col, unroll), shape((...]
    ppermute x1, starting transfers between devices: 2.44 us -> 4.04 us  [shards(): far = lax.ppermute(near, 'core', [(0, 1), (1, 0)])]
    ppermute x2, waiting for transfers between devices: 0.01 us -> 1.56 us  [shards(): lax.ppermute(array, 'pair', swap)]
    all_to_all x1, waiting for transfers between devices: 0.01 us -> 0.9 us  [shards(): lax.all_to_all(emit.reshape(half, -1), 'half', 0, 0, tiled=True)]
  transfers between devices with their start and end apart: 7 -> 7, of which waited for: 1 -> 4; matrix products, arithmetic and copies ran while one was open for 1% -> 0% of each run, Pallas kernels for 8% -> 9%
where the time goes in v4:
time: 76.3 us; the launch traced here: 75.6 us
  blocking collectives  30.1 us (39%)
  Pallas kernels  21.3 us (28%)
  starting transfers between devices  18.6 us (24%)
  waiting for transfers between devices  4.01 us (5%)
  between operations  1.49 us (2%)
    all_to_all x1, blocking collectives, shards(): part = lax.all_to_all(part.reshape(n_row, -1), ROW, 0, 0, tiled=True)  15.2 us
    all_to_all x1, blocking collectives, shards(): lax.all_to_all(message.reshape(devices, -1), AXES, 0, 0, tiled=True)  14.9 us
    pallas_call x1, Pallas kernels, shards(): call(functools.partial(pair_kernel, tiles, n_row, n_col, unroll), shape((...  11.7 us
    all_to_all x1, starting transfers between devices, shards(): lax.all_to_all(emit.reshape(half, -1), 'half', 0, 0, tiled=True)  7.31 us
    ppermute x3, starting transfers between devices, shards(): lax.ppermute(both, 'ring', [(i, (i + k) % ring) for i in range(ring)])  5.05 us
    ppermute x1, starting transfers between devices, shards(): far = lax.ppermute(near, 'core', [(0, 1), (1, 0)])  4.04 us
    pallas_call x1, Pallas kernels, shards(): call(functools.partial(rank_kernel, tiles, n_row, n_col), (shape((tiles,...  2.91 us
    ppermute x2, starting transfers between devices, shards(): lax.ppermute(array, 'pair', swap)  2.21 us
  transfers between devices with their start and end apart: 7, of which 4 were waited for; matrix products, arithmetic and copies ran while one was open for 0% of the time, Pallas kernels for 9%

profile of v4, /device:TPU:1, one launch (start us, length us, event | category | flops | bytes accessed | tf_op | source)
XLA Modules:
  0.0 75.6 jit_solution(4633373588630851836)
XLA Ops:
  0.6 0.0 copy-start.1
  0.6 0.0 copy-start.2
  0.7 2.1 %collective-permute-start = (f32[3,3072]{1,0:T(4,128)}, f32[3,3072]{1,0:T(4,128)S(1)}, u32[]{:S(2)}, u32[]{:S(2)}) collective-permute-start(f32[3,3072]{1,0:T(4,128)} %own_pos.1), channel_id=1, source_target_pairs={{0,64},{64,0},{1,65},{65,1},{2,66},{66,2},{3,67},{67,3},{4,68},{68... | collective-permute-start | bytes 110600 | tf_op jit(solution)/shard_map/ppermute | solution.py:407
  2.8 0.1 collective-permute-start.1
  2.9 2.0 %emit.1 = f32[1536,128]{1,0:T(8,128)} custom-call(f32[3,3072]{1,0:T(4,128)} %own_pos.1, f32[3,3072]{1,0:T(4,128)} %own_nor.1, f32[1,3072]{1,0:T(1,128)} %bitcast.30, f32[1,3072]{1,0:T(1,128)} %bitcast.37, f32[8,3072]{1,0:T(8,128)} %basis.7), custom_call_target="tpu_custom_call" | custom-call | flops 4400000000 | bytes 65536 | tf_op jit(solution)/shard_map/emit/pallas_call | solution.py:408
  4.8 0.0 collective-permute-done.pos
  4.9 1.6 %collective-permute-done.1.nor = f32[3,3072]{1,0:T(4,128)S(1)} collective-permute-done((f32[3,3072]{1,0:T(4,128)}, f32[3,3072]{1,0:T(4,128)S(1)}, u32[]{:S(2)}, u32[]{:S(2)}) %collective-permute-start.1) | collective-permute-done | bytes 36896 | tf_op jit(solution)/shard_map/ppermute | solution.py:407
  6.4 7.3 %all-to-all-start = ((f32[8,1,24576]{2,1,0:T(1,128)}), f32[8,1,24576]{2,1,0:T(1,128)S(1)}, u32[]{:S(2)}, u32[]{:S(2)}) async-start(f32[8,1,24576]{2,1,0:T(1,128)} %bitcast.36), calls=%async_computation | async-start | bytes 1572864 | tf_op jit(solution)/shard_map/all_to_all | solution.py:452
  13.7 0.0 copy-done.1
  13.7 0.0 copy-done.2
  13.7 0.1 join.1.refs_0_
  13.8 1.4 %collective-permute-start.2 = (f32[288,128]{1,0:T(8,128)S(1)}, f32[288,128]{1,0:T(8,128)S(1)}, u32[]{:S(2)}, u32[]{:S(2)}) collective-permute-start(f32[288,128]{1,0:T(8,128)S(1)} %join.1.refs_0_), channel_id=1, source_target_pairs={{0,16},{16,32},{32,48},{48,0},{1,17},{17,33},{33,49},{49,1},{2,18}... | collective-permute-start | bytes 442376 | tf_op jit(solution)/shard_map/ppermute | solution.py:449
  15.2 2.6 %collective-permute-start.3 = (f32[288,128]{1,0:T(8,128)S(1)}, f32[288,128]{1,0:T(8,128)S(1)}, u32[]{:S(2)}, u32[]{:S(2)}) collective-permute-start(f32[288,128]{1,0:T(8,128)S(1)} %join.1.refs_0_), channel_id=1, source_target_pairs={{0,32},{16,48},{32,0},{48,16},{1,33},{17,49},{33,1},{49,17},{2,34}... | collective-permute-start | bytes 442376 | tf_op jit(solution)/shard_map/ppermute | solution.py:449
  17.8 1.1 %collective-permute-start.4 = (f32[288,128]{1,0:T(8,128)S(1)}, f32[288,128]{1,0:T(8,128)S(1)}, u32[]{:S(2)}, u32[]{:S(2)}) collective-permute-start(f32[288,128]{1,0:T(8,128)S(1)} %join.1.refs_0_), channel_id=1, source_target_pairs={{0,48},{16,0},{32,16},{48,32},{1,49},{17,1},{33,17},{49,33},{2,50}... | collective-permute-start | bytes 442376 | tf_op jit(solution)/shard_map/ppermute | solution.py:449
  18.9 2.9 %rank.1 = (s32[24,128]{1,0:T(8,128)}, f32[128,128]{1,0:T(8,128)}, f32[1,128]{1,0:T(1,128)}, s32[4,128]{1,0:T(4,128)}, s32[4,128]{1,0:T(4,128)}) custom-call(s32[24,128]{1,0:T(8,128)} %bitcast.28, s32[24,128]{1,0:T(8,128)} %bitcast.38, f32[8,3072]{1,0:T(8,128)} %basis.7, s32[4,128]{1,0:T(4,128)} %bitcast.39, s32[4,128]{1,0:T(4,128)} %bitcast.40), custom_call_target="tpu_custom_call" | custom-call | flops 3300000000 | bytes 65536 | tf_op jit(solution)/shard_map/rank/pallas_call | solution.py:434
  21.8 0.0 copy-start.7
  21.8 0.0 copy-start.8
  21.8 0.0 collective-permute-done.2.refs_1_
  21.8 1.2 %collective-permute-done.3.refs_2_ = f32[288,128]{1,0:T(8,128)S(1)} collective-permute-done((f32[288,128]{1,0:T(8,128)S(1)}, f32[288,128]{1,0:T(8,128)S(1)}, u32[]{:S(2)}, u32[]{:S(2)}) %collective-permute-start.3) | collective-permute-done | bytes 147488 | tf_op jit(solution)/shard_map/ppermute | solution.py:449
  23.0 0.3 collective-permute-done.4.refs_3_
  23.3 0.9 %all-to-all-done = f32[8,1,24576]{2,1,0:T(1,128)S(1)} async-done(((f32[8,1,24576]{2,1,0:T(1,128)}), f32[8,1,24576]{2,1,0:T(1,128)S(1)}, u32[]{:S(2)}, u32[]{:S(2)}) %all-to-all-start) | async-done | bytes 786464 | tf_op jit(solution)/shard_map/all_to_all | solution.py:452
  24.2 4.0 %collective-permute-start.5 = (f32[1536,128]{1,0:T(8,128)S(1)}, f32[1536,128]{1,0:T(8,128)S(1)}, u32[]{:S(2)}, u32[]{:S(2)}) collective-permute-start(f32[1536,128]{1,0:T(8,128)S(1)} %bitcast.22), channel_id=1, source_target_pairs={{0,1},{1,0},{2,3},{3,2},{4,5},{5,4},{6,7},{7,6},{8,9},{9,8},{10,11... | collective-permute-start | bytes 2359304 | tf_op jit(solution)/shard_map/ppermute | solution.py:456
  28.9 1.8 %receivers.1.wtab = bf16[192,64,384]{2,1,0:T(8,128)(2,1)S(1)} custom-call(f32[288,128]{1,0:T(8,128)S(1)} %join.1.refs_0_, f32[288,128]{1,0:T(8,128)S(1)} %collective-permute-done.2.refs_1_, f32[288,128]{1,0:T(8,128)S(1)} %collective-permute-done.3.refs_2_, f32[288,128]{1,0:T(8,128)S(1)} %collective-permute-done.4.refs_3_), custom_call_target="tpu_custom_call" | custom-call | flops 4400000000 | bytes 65536 | tf_op jit(solution)/shard_map/receivers/pallas_call | solution.py:457
  30.8 0.0 collective-permute-done.5.far
  30.8 0.0 copy-done.7
  30.8 0.0 copy-done.8
  30.8 0.0 copy-start
  30.8 0.0 copy-start.3
  30.8 0.0 copy-start.4
  30.8 0.0 copy-start.5
  30.8 0.0 copy-start.6
  30.8 0.0 copy-start.9
  30.9 0.0 copy-start.10
  30.9 0.0 copy-start.11
  30.9 11.7 %pairs.1 = f32[384,128]{1,0:T(8,128)S(1)} custom-call(s32[1]{0:T(128)} %bitcast.21.count, s32[512]{0:T(512)S(1)} %bitcast.34, s32[512]{0:T(512)S(1)} %bitcast.35, f32[1536,128]{1,0:T(8,128)S(1)} %bitcast.23, f32[1536,128]{1,0:T(8,128)S(1)} %collective-permute-done.5.far, bf16[192,64,384]{2,1,0:T(8,128)(2,1)S(1)} %receivers.1.wtab), custom_call_target="tpu_custom_call" | custom-call | flops 22000001024 | bytes 65536 | tf_op jit(solution)/shard_map/pairs/pallas_call | solution.py:466
  42.6 15.2 %all_to_all.27 = f32[8,1,6144]{2,1,0:T(1,128)S(1)} all-to-all(f32[8,1,6144]{2,1,0:T(1,128)S(1)} %bitcast.25), channel_id=1, replica_groups=mesh['pair'=2,'ring'=4,'half'=8,'core'=2] {'pair','ring'}, dimensions={0} | all-to-all | bytes 393216 | tf_op jit(solution)/shard_map/all_to_all | solution.py:486
  57.8 0.0 copy-done
  57.8 0.0 copy-done.3
  57.8 0.0 copy-done.4
  57.8 0.0 copy-done.5
  57.8 0.0 copy-done.6
  57.8 0.0 copy-done.9
  57.8 0.0 copy-done.10
  57.8 0.0 copy-done.11
  57.8 0.8 %loads.1 = (f32[256,128]{1,0:T(8,128)S(1)}, f32[24,128]{1,0:T(8,128)S(1)}) custom-call(f32[384,128]{1,0:T(8,128)S(1)} %bitcast.24, f32[8,3072]{1,0:T(8,128)S(1)} %copy-done, f32[24,128]{1,0:T(8,128)S(1)} %bitcast.32, f32[24,128]{1,0:T(8,128)S(1)} %bitcast.33, f32[24,128]{1,0:T(8,128)S(1)} %bitcast.31, s32[24,128]{1,0:T(8,128)S(1)} %bitcast.29, ...), custom_call_target="tpu_custom_call" | custom-call | flops 1100000000 | bytes 65536 | tf_op jit(solution)/shard_map/loads/pallas_call | solution.py:487
  58.7 14.9 %all_to_all.28 = f32[128,1,256]{2,1,0:T(1,128)S(1)} all-to-all(f32[128,1,256]{2,1,0:T(1,128)S(1)} %bitcast.26), channel_id=1, replica_groups=mesh['pair'=2,'ring'=4,'half'=8,'core'=2] {'pair','ring','half','core'}, dimensions={0} | all-to-all | bytes 262144 | tf_op jit(solution)/shard_map/all_to_all | solution.py:503
  73.5 2.0 %finish.1 = (f32[24,128]{1,0:T(8,128)}, f32[1,9]{1,0:T(1,128)}, f32[16,128]{1,0:T(8,128)}) custom-call(f32[256,128]{1,0:T(8,128)S(1)} %bitcast.27, f32[8,3072]{1,0:T(8,128)S(1)} %copy-done, f32[24,128]{1,0:T(8,128)S(1)} %get-tuple-element.43.damped), custom_call_target="tpu_custom_call" | custom-call | flops 1100000000 | bytes 65536 | tf_op jit(solution)/shard_map/finish/pallas_call | solution.py:504
Async XLA Ops:
  0.6 13.1 %copy-start.1 = (f32[3,3072]{1,0:T(4,128)S(1)}, f32[3,3072]{1,0:T(4,128)}, u32[]{:S(2)}) copy-start(f32[3,3072]{1,0:T(4,128)} %own_pos.1) | copy-start | bytes 110596
  0.6 13.1 %copy-start.2 = (f32[3,3072]{1,0:T(4,128)S(1)}, f32[3,3072]{1,0:T(4,128)}, u32[]{:S(2)}) copy-start(f32[3,3072]{1,0:T(4,128)} %own_nor.1) | copy-start | bytes 110596
  0.7 4.2 %collective-permute-start = (f32[3,3072]{1,0:T(4,128)}, f32[3,3072]{1,0:T(4,128)S(1)}, u32[]{:S(2)}, u32[]{:S(2)}) collective-permute-start(f32[3,3072]{1,0:T(4,128)} %own_pos.1), channel_id=1, source_target_pairs={{0,64},{64,0},{1,65},{65,1},{2,66},{66,2},{3,67},{67,3},{4,68},{68... | collective-permute-start | bytes 110600 | tf_op jit(solution)/shard_map/ppermute | solution.py:407
  2.8 3.6 %collective-permute-start.1 = (f32[3,3072]{1,0:T(4,128)}, f32[3,3072]{1,0:T(4,128)S(1)}, u32[]{:S(2)}, u32[]{:S(2)}) collective-permute-start(f32[3,3072]{1,0:T(4,128)} %own_nor.1), channel_id=1, source_target_pairs={{0,64},{64,0},{1,65},{65,1},{2,66},{66,2},{3,67},{67,3},{4,68},{68... | collective-permute-start | bytes 110600 | tf_op jit(solution)/shard_map/ppermute | solution.py:407
  6.4 17.8 %all-to-all-start = ((f32[8,1,24576]{2,1,0:T(1,128)}), f32[8,1,24576]{2,1,0:T(1,128)S(1)}, u32[]{:S(2)}, u32[]{:S(2)}) async-start(f32[8,1,24576]{2,1,0:T(1,128)} %bitcast.36), calls=%async_computation | async-start | bytes 1572864 | tf_op jit(solution)/shard_map/all_to_all | solution.py:452
  13.8 8.0 %collective-permute-start.2 = (f32[288,128]{1,0:T(8,128)S(1)}, f32[288,128]{1,0:T(8,128)S(1)}, u32[]{:S(2)}, u32[]{:S(2)}) collective-permute-start(f32[288,128]{1,0:T(8,128)S(1)} %join.1.refs_0_), channel_id=1, source_target_pairs={{0,16},{16,32},{32,48},{48,0},{1,17},{17,33},{33,49},{49,1},{2,18}... | collective-permute-start | bytes 442376 | tf_op jit(solution)/shard_map/ppermute | solution.py:449
  15.2 7.9 %collective-permute-start.3 = (f32[288,128]{1,0:T(8,128)S(1)}, f32[288,128]{1,0:T(8,128)S(1)}, u32[]{:S(2)}, u32[]{:S(2)}) collective-permute-start(f32[288,128]{1,0:T(8,128)S(1)} %join.1.refs_0_), channel_id=1, source_target_pairs={{0,32},{16,48},{32,0},{48,16},{1,33},{17,49},{33,1},{49,17},{2,34}... | collective-permute-start | bytes 442376 | tf_op jit(solution)/shard_map/ppermute | solution.py:449
  17.8 5.5 %collective-permute-start.4 = (f32[288,128]{1,0:T(8,128)S(1)}, f32[288,128]{1,0:T(8,128)S(1)}, u32[]{:S(2)}, u32[]{:S(2)}) collective-permute-start(f32[288,128]{1,0:T(8,128)S(1)} %join.1.refs_0_), channel_id=1, source_target_pairs={{0,48},{16,0},{32,16},{48,32},{1,49},{17,1},{33,17},{49,33},{2,50}... | collective-permute-start | bytes 442376 | tf_op jit(solution)/shard_map/ppermute | solution.py:449
  21.8 9.0 %copy-start.7 = (s32[4,128]{1,0:T(4,128)S(1)}, s32[4,128]{1,0:T(4,128)}, u32[]{:S(2)}) copy-start(s32[4,128]{1,0:T(4,128)} %get-tuple-element.32) | copy-start | bytes 6148
  21.8 9.0 %copy-start.8 = (s32[4,128]{1,0:T(4,128)S(1)}, s32[4,128]{1,0:T(4,128)}, u32[]{:S(2)}) copy-start(s32[4,128]{1,0:T(4,128)} %get-tuple-element.33) | copy-start | bytes 6148
  24.2 6.5 %collective-permute-start.5 = (f32[1536,128]{1,0:T(8,128)S(1)}, f32[1536,128]{1,0:T(8,128)S(1)}, u32[]{:S(2)}, u32[]{:S(2)}) collective-permute-start(f32[1536,128]{1,0:T(8,128)S(1)} %bitcast.22), channel_id=1, source_target_pairs={{0,1},{1,0},{2,3},{3,2},{4,5},{5,4},{6,7},{7,6},{8,9},{9,8},{10,11... | collective-permute-start | bytes 2359304 | tf_op jit(solution)/shard_map/ppermute | solution.py:456
  30.8 27.0 %copy-start = (f32[8,3072]{1,0:T(8,128)S(1)}, f32[8,3072]{1,0:T(8,128)}, u32[]{:S(2)}) copy-start(f32[8,3072]{1,0:T(8,128)} %basis.7) | copy-start | bytes 294916
  30.8 27.0 %copy-start.3 = (s32[3072,1]{0,1:T(1,128)S(1)}, s32[3072,1]{0,1:T(1,128)}, u32[]{:S(2)}) copy-start(s32[3072,1]{0,1:T(1,128)} %param.22) | copy-start | bytes 36868
  30.8 27.0 %copy-start.4 = (f32[3072]{0:T(1024)S(1)}, f32[3072]{0:T(1024)}, u32[]{:S(2)}) copy-start(f32[3072]{0:T(1024)} %param.14) | copy-start | bytes 36868
  30.8 27.0 %copy-start.5 = (f32[3072]{0:T(1024)S(1)}, f32[3072]{0:T(1024)}, u32[]{:S(2)}) copy-start(f32[3072]{0:T(1024)} %param.15) | copy-start | bytes 36868
  30.8 27.0 %copy-start.6 = (f32[3072]{0:T(1024)S(1)}, f32[3072]{0:T(1024)}, u32[]{:S(2)}) copy-start(f32[3072]{0:T(1024)} %param.16) | copy-start | bytes 36868
  30.8 27.0 %copy-start.9 = (f32[128,128]{1,0:T(8,128)S(1)}, f32[128,128]{1,0:T(8,128)}, u32[]{:S(2)}) copy-start(f32[128,128]{1,0:T(8,128)} %get-tuple-element.40.slots) | copy-start | bytes 196612
  30.9 27.0 %copy-start.10 = (s32[24,128]{1,0:T(8,128)S(1)}, s32[24,128]{1,0:T(8,128)}, u32[]{:S(2)}) copy-start(s32[24,128]{1,0:T(8,128)} %get-tuple-element.39.rank) | copy-start | bytes 36868
  30.9 27.0 %copy-start.11 = (f32[1,128]{1,0:T(1,128)S(1)}, f32[1,128]{1,0:T(1,128)}, u32[]{:S(2)}) copy-start(f32[1,128]{1,0:T(1,128)} %get-tuple-element.41.gram) | copy-start | bytes 1540

commit v5 on v4

--- a/solution.py
+++ b/solution.py
@@ -74,14 +74,16 @@
     blocks = 2 * tiles
     for side, arrays in enumerate(((own_pos, own_nor), (pos, nor))):
         for v, array in enumerate(arrays):
-            for k in range(tiles):
-                both[pl.ds(3 * v * blocks + side * tiles + k, 3, stride=blocks), :] = array[
-                    :, k * LANES : (k + 1) * LANES
-                ]
-
-
-def rank_kernel(tiles, n_row, n_col, owner, elem, basis, recv_list, emit_list, rank, slots, gram, recv_at, emit_at):
-    my_pair, my_ring, my_core = (lax.axis_index(a) for a in ("pair", "ring", "core"))
+            for f in range(3):
+                base = (3 * v + f) * blocks + side * tiles
+                for k in range(tiles):
+                    both[base + k : base + k + 1, :] = array[
+                        f : f + 1, k * LANES : (k + 1) * LANES
+                    ]
+
+
+def rank_kernel(tiles, n_row, n_col, place, owner, elem, basis, recv_list, emit_list, rank, slots, gram, recv_at, emit_at):
+    my_pair, my_ring, my_core = place[0], place[1], place[2]
     ring = n_row // 2
     step_of = -(-65536 // tiles)
     r = recv_list[...]
@@ -129,22 +131,20 @@
 
 
 def receiver_kernel(*refs):
-    wtab, consts_of = refs[-2:]
+    wtab, features = refs[-2:]
     row = lax.broadcasted_iota(jnp.int32, (8, LANES), 0)
     zero = jnp.zeros((8, LANES), F32)
     base = 0
     for recv in refs[:-2]:
         blocks = recv.shape[0] // 6
         x = [recv[f * blocks : (f + 1) * blocks, :] for f in range(6)]
-        consts_of[0] = -(x[0] * x[3] + x[1] * x[4] + x[2] * x[5])
-        consts_of[1] = x[0] * x[0] + x[1] * x[1] + x[2] * x[2]
+        x.append(-(x[0] * x[3] + x[1] * x[4] + x[2] * x[5]))
+        x.append(x[0] * x[0] + x[1] * x[1] + x[2] * x[2])
+        for f in range(8):
+            features[pl.ds(f, blocks, stride=8), :] = x[f]
 
         def body(k, _):
-            block = jnp.concatenate(
-                [recv[pl.ds(k, 6, stride=blocks), :]]
-                + [consts_of[f, pl.ds(k, 1), :] for f in range(2)],
-                0,
-            )
+            block = features[pl.ds(pl.multiple_of(k * 8, 8), 8), :]
             parts = split3(block)
             facing, away, spread = [], [], []
             for p, part in enumerate(parts):
@@ -173,7 +173,7 @@
         base += blocks
 
 
-def pair_kernel(tiles, n_row, n_col, unroll, count, recv_list, emit_list, near, far, wtab, out, etab, along, ratio, acc):
+def pair_kernel(tiles, n_row, n_col, unroll, count, recv_list, emit_list, place, near, far, wtab, out, etab, along, ratio, acc):
     row = lax.broadcasted_iota(jnp.int32, (8, LANES), 0)
     ones3 = jnp.where(row < 3, 1.0, 0.0)
     half = n_col // 2
@@ -217,7 +217,7 @@
             total = total + full[8 * k : 8 * k + 8]
         return total
 
-    my_pair, my_ring = lax.axis_index("pair"), lax.axis_index("ring")
+    my_pair, my_ring = place[0], place[1]
     ring = n_row // 2
 
     empty = jnp.zeros((64, 3 * LANES), BF16)
@@ -397,6 +397,7 @@
     pairs_of, ring, half, cores = (lax.axis_size(a) for a in AXES)
     n_row, n_col = pairs_of * ring, half * cores
     devices = n_row * n_col
+    place = jnp.stack([lax.axis_index(a) for a in ("pair", "ring", "core")])
     shape = jax.ShapeDtypeStruct
 
     def rows(array):
@@ -421,7 +422,6 @@
         micros=4,
         limit=60 * 2**20,
     )(positions, normals, patch_extents[None], radiosity[None], basis)
-    emit, swapped = lax.optimization_barrier((emit, swapped))
     both = call(
         functools.partial(join_kernel, tiles),
         shape((12 * tiles, LANES), F32),
@@ -440,11 +440,11 @@
             shape(lists[0].shape, jnp.int32),
             shape(lists[1].shape, jnp.int32),
         ),
-        in_specs=[VMEM] * 5,
+        in_specs=[SMEM] + [VMEM] * 5,
         name="rank",
         micros=3,
         limit=60 * 2**20,
-    )(owner_rows, rows(local_elem), basis, *lists)
+    )(place, owner_rows, rows(local_elem), basis, *lists)
     received = [both_again] + [
         lax.ppermute(both, "ring", [(i, (i + k) % ring) for i in range(ring)])
         for k in range(1, ring)
@@ -457,7 +457,7 @@
     wtab = call(
         receiver_kernel,
         shape((n_row * tiles, 64, 3 * LANES), BF16),
-        scratch=[pltpu.VMEM((2, 2 * tiles, LANES), F32)],
+        scratch=[pltpu.VMEM((16 * tiles, LANES), F32)],
         in_specs=[VMEM] * len(received),
         name="receivers",
         micros=4,
@@ -472,13 +472,14 @@
             pltpu.VMEM((n_col * tiles // LANES, LANES, LANES), F32),
             pltpu.VMEM((n_row * tiles * 16, LANES), F32),
         ],
-        in_specs=[SMEM] * 3 + [VMEM] * 3,
+        in_specs=[SMEM] * 4 + [VMEM] * 3,
         name="pairs",
         micros=20,
     )(
         vis_count.reshape(-1),
         recv_at.reshape(-1),
         emit_at.reshape(-1),
+        place,
         near,
         far,
         wtab,

time: 76.3 us -> 76.5 us (level)
  blocking collectives: 30.1 us -> 35.9 us
  Pallas kernels: 21.3 us -> 17.4 us
  waiting for transfers between devices: 4.01 us -> 2.01 us
    all_to_all x1, blocking collectives: 15.2 us -> 19.3 us  [shards(): part = lax.all_to_all(part.reshape(n_row, -1), ROW, 0, 0, tiled=True)]
    pallas_call x1, Pallas kernels: 11.7 us -> 7.92 us  [shards(): call(functools.partial(pair_kernel, tiles, n_row, n_col, unroll), shape((...]
    all_to_all x1, blocking collectives: 14.9 us -> 16.5 us  [shards(): lax.all_to_all(message.reshape(devices, -1), AXES, 0, 0, tiled=True)]
    ppermute x2, waiting for transfers between devices: 1.56 us -> 0.01 us  [shards(): lax.ppermute(array, 'pair', swap)]
  transfers between devices with their start and end apart: 7 -> 7, of which waited for: 4 -> 3; matrix products, arithmetic and copies ran while one was open for 0% -> 1% of each run, Pallas kernels for 9% -> 9%
where the time goes in v5:
time: 76.5 us; the launch traced here: 76.1 us
  blocking collectives  35.9 us (47%)
  starting transfers between devices  18.5 us (24%)
  Pallas kernels  17.4 us (23%)
  waiting for transfers between devices  2.01 us (3%)
  between operations  1.51 us (2%)
    all_to_all x1, blocking collectives, shards(): part = lax.all_to_all(part.reshape(n_row, -1), ROW, 0, 0, tiled=True)  19.3 us
    all_to_all x1, blocking collectives, shards(): lax.all_to_all(message.reshape(devices, -1), AXES, 0, 0, tiled=True)  16.5 us
    pallas_call x1, Pallas kernels, shards(): call(functools.partial(pair_kernel, tiles, n_row, n_col, unroll), shape((...  7.92 us
    all_to_all x1, starting transfers between devices, shards(): lax.all_to_all(emit.reshape(half, -1), 'half', 0, 0, tiled=True)  7.67 us
    ppermute x3, starting transfers between devices, shards(): lax.ppermute(both, 'ring', [(i, (i + k) % ring) for i in range(ring)])  5.05 us
    ppermute x1, starting transfers between devices, shards(): far = lax.ppermute(near, 'core', [(0, 1), (1, 0)])  3.6 us
    pallas_call x1, Pallas kernels, shards(): call(functools.partial(rank_kernel, tiles, n_row, n_col), (shape((tiles,...  2.91 us
    ppermute x2, starting transfers between devices, shards(): lax.ppermute(array, 'pair', swap)  2.21 us
  transfers between devices with their start and end apart: 7, of which 3 were waited for; matrix products, arithmetic and copies ran while one was open for 1% of the time, Pallas kernels for 9%

profile of v5, /device:TPU:1, one launch (start us, length us, event | category | flops | bytes accessed | tf_op | source)
XLA Modules:
  0.0 76.1 jit_solution(6347627833732099282)
XLA Ops:
  0.6 0.0 copy-start.2
  0.6 0.0 copy-start.3
  0.7 2.1 %collective-permute-start = (f32[3,3072]{1,0:T(4,128)}, f32[3,3072]{1,0:T(4,128)S(1)}, u32[]{:S(2)}, u32[]{:S(2)}) collective-permute-start(f32[3,3072]{1,0:T(4,128)} %own_pos.1), channel_id=1, source_target_pairs={{0,64},{64,0},{1,65},{65,1},{2,66},{66,2},{3,67},{67,3},{4,68},{68... | collective-permute-start | bytes 110600 | tf_op jit(solution)/shard_map/ppermute | solution.py:408
  2.8 0.1 collective-permute-start.1
  2.9 2.0 %emit.1 = f32[1536,128]{1,0:T(8,128)} custom-call(f32[3,3072]{1,0:T(4,128)} %own_pos.1, f32[3,3072]{1,0:T(4,128)} %own_nor.1, f32[1,3072]{1,0:T(1,128)} %bitcast.33, f32[1,3072]{1,0:T(1,128)} %bitcast.40, f32[8,3072]{1,0:T(8,128)} %basis.7), custom_call_target="tpu_custom_call" | custom-call | flops 4400000000 | bytes 65536 | tf_op jit(solution)/shard_map/emit/pallas_call | solution.py:409
  4.8 7.7 %all-to-all-start = ((f32[8,1,24576]{2,1,0:T(1,128)}), f32[8,1,24576]{2,1,0:T(1,128)S(1)}, u32[]{:S(2)}, u32[]{:S(2)}) async-start(f32[8,1,24576]{2,1,0:T(1,128)} %bitcast.39), calls=%async_computation | async-start | bytes 1572864 | tf_op jit(solution)/shard_map/all_to_all | solution.py:452
  12.5 0.7 pad_add_fusion.place
  13.2 0.0 collective-permute-done.pos
  13.2 0.0 collective-permute-done.1.nor
  13.2 0.0 copy-done.2
  13.2 0.0 copy-done.3
  13.2 0.1 join.1.refs_0_
  13.3 1.4 %collective-permute-start.2 = (f32[288,128]{1,0:T(8,128)S(1)}, f32[288,128]{1,0:T(8,128)S(1)}, u32[]{:S(2)}, u32[]{:S(2)}) collective-permute-start(f32[288,128]{1,0:T(8,128)S(1)} %join.1.refs_0_), channel_id=1, source_target_pairs={{0,16},{16,32},{32,48},{48,0},{1,17},{17,33},{33,49},{49,1},{2,18}... | collective-permute-start | bytes 442376 | tf_op jit(solution)/shard_map/ppermute | solution.py:449
  14.7 2.6 %collective-permute-start.3 = (f32[288,128]{1,0:T(8,128)S(1)}, f32[288,128]{1,0:T(8,128)S(1)}, u32[]{:S(2)}, u32[]{:S(2)}) collective-permute-start(f32[288,128]{1,0:T(8,128)S(1)} %join.1.refs_0_), channel_id=1, source_target_pairs={{0,32},{16,48},{32,0},{48,16},{1,33},{17,49},{33,1},{49,17},{2,34}... | collective-permute-start | bytes 442376 | tf_op jit(solution)/shard_map/ppermute | solution.py:449
  17.3 1.1 %collective-permute-start.4 = (f32[288,128]{1,0:T(8,128)S(1)}, f32[288,128]{1,0:T(8,128)S(1)}, u32[]{:S(2)}, u32[]{:S(2)}) collective-permute-start(f32[288,128]{1,0:T(8,128)S(1)} %join.1.refs_0_), channel_id=1, source_target_pairs={{0,48},{16,0},{32,16},{48,32},{1,49},{17,1},{33,17},{49,33},{2,50}... | collective-permute-start | bytes 442376 | tf_op jit(solution)/shard_map/ppermute | solution.py:449
  18.4 2.9 %rank.1 = (s32[24,128]{1,0:T(8,128)}, f32[128,128]{1,0:T(8,128)}, f32[1,128]{1,0:T(1,128)}, s32[4,128]{1,0:T(4,128)}, s32[4,128]{1,0:T(4,128)}) custom-call(s32[3]{0:T(128)} %pad_add_fusion.place, s32[24,128]{1,0:T(8,128)} %bitcast.31, s32[24,128]{1,0:T(8,128)} %bitcast.41, f32[8,3072]{1,0:T(8,128)} %basis.7, s32[4,128]{1,0:T(4,128)} %bitcast.42, ...), custom_call_target="tpu_custom_call" | custom-call | flops 3300000000 | bytes 65536 | tf_op jit(solution)/shard_map/rank/pallas_call | solution.py:434
  21.3 0.0 copy-start
  21.3 0.0 copy-start.8
  21.3 0.0 copy-start.9
  21.3 0.0 collective-permute-done.2.refs_1_
  21.3 1.2 %collective-permute-done.3.refs_2_ = f32[288,128]{1,0:T(8,128)S(1)} collective-permute-done((f32[288,128]{1,0:T(8,128)S(1)}, f32[288,128]{1,0:T(8,128)S(1)}, u32[]{:S(2)}, u32[]{:S(2)}) %collective-permute-start.3) | collective-permute-done | bytes 147488 | tf_op jit(solution)/shard_map/ppermute | solution.py:449
  22.5 0.5 collective-permute-done.4.refs_3_
  23.0 0.3 all-to-all-done
  23.3 3.6 %collective-permute-start.5 = (f32[1536,128]{1,0:T(8,128)S(1)}, f32[1536,128]{1,0:T(8,128)S(1)}, u32[]{:S(2)}, u32[]{:S(2)}) collective-permute-start(f32[1536,128]{1,0:T(8,128)S(1)} %bitcast.25), channel_id=1, source_target_pairs={{0,1},{1,0},{2,3},{3,2},{4,5},{5,4},{6,7},{7,6},{8,9},{9,8},{10,11... | collective-permute-start | bytes 2359304 | tf_op jit(solution)/shard_map/ppermute | solution.py:456
  27.6 1.7 %receivers.1.wtab = bf16[192,64,384]{2,1,0:T(8,128)(2,1)S(1)} custom-call(f32[288,128]{1,0:T(8,128)S(1)} %join.1.refs_0_, f32[288,128]{1,0:T(8,128)S(1)} %collective-permute-done.2.refs_1_, f32[288,128]{1,0:T(8,128)S(1)} %collective-permute-done.3.refs_2_, f32[288,128]{1,0:T(8,128)S(1)} %collective-permute-done.4.refs_3_), custom_call_target="tpu_custom_call" | custom-call | flops 4400000000 | bytes 65536 | tf_op jit(solution)/shard_map/receivers/pallas_call | solution.py:457
  29.2 0.0 collective-permute-done.5.far
  29.2 0.0 copy-done
  29.3 0.0 copy-done.8
  29.3 0.0 copy-done.9
  29.3 0.0 copy-start.1
  29.3 0.0 copy-start.4
  29.3 0.0 copy-start.5
  29.3 0.0 copy-start.6
  29.3 0.0 copy-start.7
  29.3 0.0 copy-start.10
  29.3 0.0 copy-start.11
  29.4 0.0 copy-start.12
  29.4 7.9 %pairs.1 = f32[384,128]{1,0:T(8,128)S(1)} custom-call(s32[1]{0:T(128)} %bitcast.24.count, s32[512]{0:T(512)S(1)} %bitcast.37, s32[512]{0:T(512)S(1)} %bitcast.38, s32[3]{0:T(128)S(1)} %copy-done, f32[1536,128]{1,0:T(8,128)S(1)} %bitcast.26, f32[1536,128]{1,0:T(8,128)S(1)} %collective-permute-done.5.far, bf16[192,64,384]{2,1,0:T(8,128)(2,1)S(1)} %receivers.1.wtab), custom_call_target="tpu_custom_call" | custom-call | flops 22000001024 | bytes 65536 | tf_op jit(solution)/shard_map/pairs/pallas_call | solution.py:466
  37.3 19.3 %all_to_all.27 = f32[8,1,6144]{2,1,0:T(1,128)S(1)} all-to-all(f32[8,1,6144]{2,1,0:T(1,128)S(1)} %bitcast.27), channel_id=1, replica_groups=mesh['pair'=2,'ring'=4,'half'=8,'core'=2] {'pair','ring'}, dimensions={0} | all-to-all | bytes 393216 | tf_op jit(solution)/shard_map/all_to_all | solution.py:487
  56.6 0.0 copy-done.1
  56.6 0.0 copy-done.4
  56.6 0.0 copy-done.5
  56.7 0.0 copy-done.6
  56.7 0.0 copy-done.7
  56.7 0.0 copy-done.10
  56.7 0.0 copy-done.11
  56.7 0.0 copy-done.12
  56.7 0.8 %loads.1 = (f32[256,128]{1,0:T(8,128)S(1)}, f32[24,128]{1,0:T(8,128)S(1)}) custom-call(f32[384,128]{1,0:T(8,128)S(1)} %bitcast.28, f32[8,3072]{1,0:T(8,128)S(1)} %copy-done.1, f32[24,128]{1,0:T(8,128)S(1)} %bitcast.35, f32[24,128]{1,0:T(8,128)S(1)} %bitcast.36, f32[24,128]{1,0:T(8,128)S(1)} %bitcast.34, s32[24,128]{1,0:T(8,128)S(1)} %bitcast.32, ...), custom_call_target="tpu_custom_call" | custom-call | flops 1100000000 | bytes 65536 | tf_op jit(solution)/shard_map/loads/pallas_call | solution.py:488
  57.5 16.5 %all_to_all.28 = f32[128,1,256]{2,1,0:T(1,128)S(1)} all-to-all(f32[128,1,256]{2,1,0:T(1,128)S(1)} %bitcast.29), channel_id=1, replica_groups=mesh['pair'=2,'ring'=4,'half'=8,'core'=2] {'pair','ring','half','core'}, dimensions={0} | all-to-all | bytes 262144 | tf_op jit(solution)/shard_map/all_to_all | solution.py:504
  74.1 2.0 %finish.1 = (f32[24,128]{1,0:T(8,128)}, f32[1,9]{1,0:T(1,128)}, f32[16,128]{1,0:T(8,128)}) custom-call(f32[256,128]{1,0:T(8,128)S(1)} %bitcast.30, f32[8,3072]{1,0:T(8,128)S(1)} %copy-done.1, f32[24,128]{1,0:T(8,128)S(1)} %get-tuple-element.37.damped), custom_call_target="tpu_custom_call" | custom-call | flops 1100000000 | bytes 65536 | tf_op jit(solution)/shard_map/finish/pallas_call | solution.py:505
Async XLA Ops:
  0.6 12.6 %copy-start.2 = (f32[3,3072]{1,0:T(4,128)S(1)}, f32[3,3072]{1,0:T(4,128)}, u32[]{:S(2)}) copy-start(f32[3,3072]{1,0:T(4,128)} %own_pos.1) | copy-start | bytes 110596
  0.6 12.5 %copy-start.3 = (f32[3,3072]{1,0:T(4,128)S(1)}, f32[3,3072]{1,0:T(4,128)}, u32[]{:S(2)}) copy-start(f32[3,3072]{1,0:T(4,128)} %own_nor.1) | copy-start | bytes 110596
  0.7 12.5 %collective-permute-start = (f32[3,3072]{1,0:T(4,128)}, f32[3,3072]{1,0:T(4,128)S(1)}, u32[]{:S(2)}, u32[]{:S(2)}) collective-permute-start(f32[3,3072]{1,0:T(4,128)} %own_pos.1), channel_id=1, source_target_pairs={{0,64},{64,0},{1,65},{65,1},{2,66},{66,2},{3,67},{67,3},{4,68},{68... | collective-permute-start | bytes 110600 | tf_op jit(solution)/shard_map/ppermute | solution.py:408
  2.8 10.4 %collective-permute-start.1 = (f32[3,3072]{1,0:T(4,128)}, f32[3,3072]{1,0:T(4,128)S(1)}, u32[]{:S(2)}, u32[]{:S(2)}) collective-permute-start(f32[3,3072]{1,0:T(4,128)} %own_nor.1), channel_id=1, source_target_pairs={{0,64},{64,0},{1,65},{65,1},{2,66},{66,2},{3,67},{67,3},{4,68},{68... | collective-permute-start | bytes 110600 | tf_op jit(solution)/shard_map/ppermute | solution.py:408
  4.8 18.5 %all-to-all-start = ((f32[8,1,24576]{2,1,0:T(1,128)}), f32[8,1,24576]{2,1,0:T(1,128)S(1)}, u32[]{:S(2)}, u32[]{:S(2)}) async-start(f32[8,1,24576]{2,1,0:T(1,128)} %bitcast.39), calls=%async_computation | async-start | bytes 1572864 | tf_op jit(solution)/shard_map/all_to_all | solution.py:452
  13.3 8.0 %collective-permute-start.2 = (f32[288,128]{1,0:T(8,128)S(1)}, f32[288,128]{1,0:T(8,128)S(1)}, u32[]{:S(2)}, u32[]{:S(2)}) collective-permute-start(f32[288,128]{1,0:T(8,128)S(1)} %join.1.refs_0_), channel_id=1, source_target_pairs={{0,16},{16,32},{32,48},{48,0},{1,17},{17,33},{33,49},{49,1},{2,18}... | collective-permute-start | bytes 442376 | tf_op jit(solution)/shard_map/ppermute | solution.py:449
  14.7 7.8 %collective-permute-start.3 = (f32[288,128]{1,0:T(8,128)S(1)}, f32[288,128]{1,0:T(8,128)S(1)}, u32[]{:S(2)}, u32[]{:S(2)}) collective-permute-start(f32[288,128]{1,0:T(8,128)S(1)} %join.1.refs_0_), channel_id=1, source_target_pairs={{0,32},{16,48},{32,0},{48,16},{1,33},{17,49},{33,1},{49,17},{2,34}... | collective-permute-start | bytes 442376 | tf_op jit(solution)/shard_map/ppermute | solution.py:449
  17.3 5.7 %collective-permute-start.4 = (f32[288,128]{1,0:T(8,128)S(1)}, f32[288,128]{1,0:T(8,128)S(1)}, u32[]{:S(2)}, u32[]{:S(2)}) collective-permute-start(f32[288,128]{1,0:T(8,128)S(1)} %join.1.refs_0_), channel_id=1, source_target_pairs={{0,48},{16,0},{32,16},{48,32},{1,49},{17,1},{33,17},{49,33},{2,50}... | collective-permute-start | bytes 442376 | tf_op jit(solution)/shard_map/ppermute | solution.py:449
  21.3 8.0 %copy-start = (s32[3]{0:T(128)S(1)}, s32[3]{0:T(128)}, u32[]{:S(2)}) copy-start(s32[3]{0:T(128)} %pad_add_fusion.place) | copy-start | bytes 40
  21.3 8.0 %copy-start.8 = (s32[4,128]{1,0:T(4,128)S(1)}, s32[4,128]{1,0:T(4,128)}, u32[]{:S(2)}) copy-start(s32[4,128]{1,0:T(4,128)} %get-tuple-element.26) | copy-start | bytes 6148
  21.3 8.0 %copy-start.9 = (s32[4,128]{1,0:T(4,128)S(1)}, s32[4,128]{1,0:T(4,128)}, u32[]{:S(2)}) copy-start(s32[4,128]{1,0:T(4,128)} %get-tuple-element.27) | copy-start | bytes 6148
  23.3 5.9 %collective-permute-start.5 = (f32[1536,128]{1,0:T(8,128)S(1)}, f32[1536,128]{1,0:T(8,128)S(1)}, u32[]{:S(2)}, u32[]{:S(2)}) collective-permute-start(f32[1536,128]{1,0:T(8,128)S(1)} %bitcast.25), channel_id=1, source_target_pairs={{0,1},{1,0},{2,3},{3,2},{4,5},{5,4},{6,7},{7,6},{8,9},{9,8},{10,11... | collective-permute-start | bytes 2359304 | tf_op jit(solution)/shard_map/ppermute | solution.py:456
  29.3 27.4 %copy-start.1 = (f32[8,3072]{1,0:T(8,128)S(1)}, f32[8,3072]{1,0:T(8,128)}, u32[]{:S(2)}) copy-start(f32[8,3072]{1,0:T(8,128)} %basis.7) | copy-start | bytes 294916
  29.3 27.4 %copy-start.4 = (s32[3072,1]{0,1:T(1,128)S(1)}, s32[3072,1]{0,1:T(1,128)}, u32[]{:S(2)}) copy-start(s32[3072,1]{0,1:T(1,128)} %param.22) | copy-start | bytes 36868
  29.3 27.3 %copy-start.5 = (f32[3072]{0:T(1024)S(1)}, f32[3072]{0:T(1024)}, u32[]{:S(2)}) copy-start(f32[3072]{0:T(1024)} %param.14) | copy-start | bytes 36868
  29.3 27.3 %copy-start.6 = (f32[3072]{0:T(1024)S(1)}, f32[3072]{0:T(1024)}, u32[]{:S(2)}) copy-start(f32[3072]{0:T(1024)} %param.15) | copy-start | bytes 36868
  29.3 27.3 %copy-start.7 = (f32[3072]{0:T(1024)S(1)}, f32[3072]{0:T(1024)}, u32[]{:S(2)}) copy-start(f32[3072]{0:T(1024)} %param.16) | copy-start | bytes 36868
  29.3 27.3 %copy-start.10 = (f32[128,128]{1,0:T(8,128)S(1)}, f32[128,128]{1,0:T(8,128)}, u32[]{:S(2)}) copy-start(f32[128,128]{1,0:T(8,128)} %get-tuple-element.34.slots) | copy-start | bytes 196612
  29.3 27.3 %copy-start.11 = (s32[24,128]{1,0:T(8,128)S(1)}, s32[24,128]{1,0:T(8,128)}, u32[]{:S(2)}) copy-start(s32[24,128]{1,0:T(8,128)} %get-tuple-element.33.rank) | copy-start | bytes 36868
  29.4 27.3 %copy-start.12 = (f32[1,128]{1,0:T(1,128)S(1)}, f32[1,128]{1,0:T(1,128)}, u32[]{:S(2)}) copy-start(f32[1,128]{1,0:T(1,128)} %get-tuple-element.35.gram) | copy-start | bytes 1540

commit v6 on v5

--- a/solution.py
+++ b/solution.py
@@ -313,7 +313,7 @@
     message[pl.ds(1, LANES, stride=2), :] = jnp.where(keep, slots[...], more)
 
 
-def finish_kernel(tiles, cells, arrived, basis, damped, vector, hessen, loads, value_rows, index_rows):
+def finish_kernel(tiles, cells, arrived, basis, damped, vector, hessen, loads, value_rows, high_rows, low_rows):
     values = arrived[pl.ds(0, LANES, stride=2), :]
     second = arrived[pl.ds(1, LANES, stride=2), :]
     top = jnp.sum(values, axis=0, keepdims=True)
@@ -354,27 +354,48 @@
     keep = lax.broadcasted_iota(jnp.int32, (LANES, LANES), 1) < 96
     for k, v in enumerate(split3(jnp.where(keep, values, 0.0))):
         value_rows[k] = v
-    index_rows[...] = second.astype(jnp.int32)
-    sub = lax.broadcasted_iota(jnp.int32, (LANES, LANES), 0)
-    sub16 = lax.broadcasted_iota(jnp.int32, (16, LANES), 0)
-    total = jnp.zeros((48, LANES), F32)
+    index = second.astype(jnp.int32)
+    high_rows[...] = (index >> 7).astype(F32)
+    low_rows[...] = (index & 127).astype(F32)
+    sub = lax.broadcasted_iota(jnp.int32, (LANES, LANES), 0).astype(F32).astype(BF16)
+    sub16 = sub[0:16]
+    one, none = jnp.ones((16, LANES), BF16), jnp.zeros((16, LANES), BF16)
+
+    def wide(row):
+        return jnp.broadcast_to(row, (16, LANES)).astype(BF16)
+
+    total = jnp.zeros((LANES, 48), F32)
     for s in range(0, LANES, 8):
         left_side, right_side = [], []
         for u in range(s, s + 8):
-            index = index_rows[u : u + 1, :]
-            mask = (index >> 7) == sub16
+            high = wide(high_rows[u : u + 1, :])
+            low = wide(low_rows[u : u + 1, :])
+            mask = high == sub16
             left_side.append(
                 jnp.concatenate(
-                    [jnp.where(mask, value_rows[k, u : u + 1, :], 0.0) for k in range(3)], 0
-                ).astype(BF16)
+                    [
+                        jnp.where(mask, wide(value_rows[k, u : u + 1, :]), none)
+                        for k in range(3)
+                    ],
+                    0,
+                )
             )
-            right_side.append(jnp.where((index & 127) == sub, 1.0, 0.0).astype(BF16))
+            right_side.append(
+                jnp.concatenate(
+                    [
+                        jnp.where(low == sub[k : k + 16], one, none)
+                        for k in range(0, LANES, 16)
+                    ],
+                    0,
+                )
+            )
         total = total + lax.dot_general(
+            jnp.concatenate(right_side, 1),
             jnp.concatenate(left_side, 1),
-            jnp.concatenate(right_side, 1),
             NT,
             preferred_element_type=F32,
         )
+    total = total.T
     loads[...] = total[0:16] + total[16:32] + total[32:48]
 
 
@@ -509,7 +530,7 @@
             shape((1, 9), F32),
             shape((E_DEV // LANES, LANES), F32),
         ),
-        scratch=[pltpu.VMEM((3, LANES, LANES), F32), pltpu.VMEM((LANES, LANES), jnp.int32)],
+        scratch=[pltpu.VMEM((3, LANES, LANES), F32)] + [pltpu.VMEM((LANES, LANES), F32)] * 2,
         in_specs=[VMEM] * 3,
         name="finish",
     )(rows(arrived), basis, damped)

time: 76.5 us -> 75.8 us (level)
  blocking collectives: 35.9 us -> 32.8 us
  Pallas kernels: 17.4 us -> 19.2 us
    all_to_all x1, blocking collectives: 19.3 us -> 13.9 us  [shards(): part = lax.all_to_all(part.reshape(n_row, -1), ROW, 0, 0, tiled=True)]
    all_to_all x1, blocking collectives: 16.5 us -> 18.9 us  [shards(): lax.all_to_all(message.reshape(devices, -1), AXES, 0, 0, tiled=True)]
    pallas_call x1, Pallas kernels: 7.92 us -> 9.81 us  [shards(): call(functools.partial(pair_kernel, tiles, n_row, n_col, unroll), shape((...]
where the time goes in v6:
time: 75.8 us; the launch traced here: 74.8 us
  blocking collectives  32.8 us (43%)
  Pallas kernels  19.2 us (25%)
  starting transfers between devices  18.5 us (24%)
  waiting for transfers between devices  2.01 us (3%)
  between operations  1.51 us (2%)
    all_to_all x1, blocking collectives, shards(): lax.all_to_all(message.reshape(devices, -1), AXES, 0, 0, tiled=True)  18.9 us
    all_to_all x1, blocking collectives, shards(): part = lax.all_to_all(part.reshape(n_row, -1), ROW, 0, 0, tiled=True)  13.9 us
    pallas_call x1, Pallas kernels, shards(): call(functools.partial(pair_kernel, tiles, n_row, n_col, unroll), shape((...  9.81 us
    all_to_all x1, starting transfers between devices, shards(): lax.all_to_all(emit.reshape(half, -1), 'half', 0, 0, tiled=True)  7.67 us
    ppermute x3, starting transfers between devices, shards(): lax.ppermute(both, 'ring', [(i, (i + k) % ring) for i in range(ring)])  5.05 us
    ppermute x1, starting transfers between devices, shards(): far = lax.ppermute(near, 'core', [(0, 1), (1, 0)])  3.6 us
    pallas_call x1, Pallas kernels, shards(): call(functools.partial(rank_kernel, tiles, n_row, n_col), (shape((tiles,...  2.91 us
    ppermute x2, starting transfers between devices, shards(): lax.ppermute(array, 'pair', swap)  2.21 us
  transfers between devices with their start and end apart: 7, of which 3 were waited for; matrix products, arithmetic and copies ran while one was open for 1% of the time, Pallas kernels for 9%

profile of v6, /device:TPU:1, one launch (start us, length us, event | category | flops | bytes accessed | tf_op | source)
XLA Modules:
  0.0 74.8 jit_solution(4206451394617186605)
XLA Ops:
  0.6 0.0 copy-start.2
  0.6 0.0 copy-start.3
  0.7 2.1 %collective-permute-start = (f32[3,3072]{1,0:T(4,128)}, f32[3,3072]{1,0:T(4,128)S(1)}, u32[]{:S(2)}, u32[]{:S(2)}) collective-permute-start(f32[3,3072]{1,0:T(4,128)} %own_pos.1), channel_id=1, source_target_pairs={{0,64},{64,0},{1,65},{65,1},{2,66},{66,2},{3,67},{67,3},{4,68},{68... | collective-permute-start | bytes 110600 | tf_op jit(solution)/shard_map/ppermute | solution.py:429
  2.8 0.1 collective-permute-start.1
  2.9 2.0 %emit.1 = f32[1536,128]{1,0:T(8,128)} custom-call(f32[3,3072]{1,0:T(4,128)} %own_pos.1, f32[3,3072]{1,0:T(4,128)} %own_nor.1, f32[1,3072]{1,0:T(1,128)} %bitcast.33, f32[1,3072]{1,0:T(1,128)} %bitcast.40, f32[8,3072]{1,0:T(8,128)} %basis.7), custom_call_target="tpu_custom_call" | custom-call | flops 4400000000 | bytes 65536 | tf_op jit(solution)/shard_map/emit/pallas_call | solution.py:430
  4.8 7.7 %all-to-all-start = ((f32[8,1,24576]{2,1,0:T(1,128)}), f32[8,1,24576]{2,1,0:T(1,128)S(1)}, u32[]{:S(2)}, u32[]{:S(2)}) async-start(f32[8,1,24576]{2,1,0:T(1,128)} %bitcast.39), calls=%async_computation | async-start | bytes 1572864 | tf_op jit(solution)/shard_map/all_to_all | solution.py:473
  12.5 0.7 pad_add_fusion.place
  13.2 0.0 collective-permute-done.pos
  13.2 0.0 collective-permute-done.1.nor
  13.2 0.0 copy-done.2
  13.2 0.0 copy-done.3
  13.2 0.1 join.1.refs_0_
  13.3 1.4 %collective-permute-start.2 = (f32[288,128]{1,0:T(8,128)S(1)}, f32[288,128]{1,0:T(8,128)S(1)}, u32[]{:S(2)}, u32[]{:S(2)}) collective-permute-start(f32[288,128]{1,0:T(8,128)S(1)} %join.1.refs_0_), channel_id=1, source_target_pairs={{0,16},{16,32},{32,48},{48,0},{1,17},{17,33},{33,49},{49,1},{2,18}... | collective-permute-start | bytes 442376 | tf_op jit(solution)/shard_map/ppermute | solution.py:470
  14.7 2.6 %collective-permute-start.3 = (f32[288,128]{1,0:T(8,128)S(1)}, f32[288,128]{1,0:T(8,128)S(1)}, u32[]{:S(2)}, u32[]{:S(2)}) collective-permute-start(f32[288,128]{1,0:T(8,128)S(1)} %join.1.refs_0_), channel_id=1, source_target_pairs={{0,32},{16,48},{32,0},{48,16},{1,33},{17,49},{33,1},{49,17},{2,34}... | collective-permute-start | bytes 442376 | tf_op jit(solution)/shard_map/ppermute | solution.py:470
  17.3 1.1 %collective-permute-start.4 = (f32[288,128]{1,0:T(8,128)S(1)}, f32[288,128]{1,0:T(8,128)S(1)}, u32[]{:S(2)}, u32[]{:S(2)}) collective-permute-start(f32[288,128]{1,0:T(8,128)S(1)} %join.1.refs_0_), channel_id=1, source_target_pairs={{0,48},{16,0},{32,16},{48,32},{1,49},{17,1},{33,17},{49,33},{2,50}... | collective-permute-start | bytes 442376 | tf_op jit(solution)/shard_map/ppermute | solution.py:470
  18.4 2.9 %rank.1 = (s32[24,128]{1,0:T(8,128)}, f32[128,128]{1,0:T(8,128)}, f32[1,128]{1,0:T(1,128)}, s32[4,128]{1,0:T(4,128)}, s32[4,128]{1,0:T(4,128)}) custom-call(s32[3]{0:T(128)} %pad_add_fusion.place, s32[24,128]{1,0:T(8,128)} %bitcast.31, s32[24,128]{1,0:T(8,128)} %bitcast.41, f32[8,3072]{1,0:T(8,128)} %basis.7, s32[4,128]{1,0:T(4,128)} %bitcast.42, ...), custom_call_target="tpu_custom_call" | custom-call | flops 3300000000 | bytes 65536 | tf_op jit(solution)/shard_map/rank/pallas_call | solution.py:455
  21.3 0.0 copy-start
  21.3 0.0 copy-start.8
  21.3 0.0 copy-start.9
  21.3 0.0 collective-permute-done.2.refs_1_
  21.3 1.2 %collective-permute-done.3.refs_2_ = f32[288,128]{1,0:T(8,128)S(1)} collective-permute-done((f32[288,128]{1,0:T(8,128)S(1)}, f32[288,128]{1,0:T(8,128)S(1)}, u32[]{:S(2)}, u32[]{:S(2)}) %collective-permute-start.3) | collective-permute-done | bytes 147488 | tf_op jit(solution)/shard_map/ppermute | solution.py:470
  22.5 0.5 collective-permute-done.4.refs_3_
  23.0 0.3 all-to-all-done
  23.3 3.6 %collective-permute-start.5 = (f32[1536,128]{1,0:T(8,128)S(1)}, f32[1536,128]{1,0:T(8,128)S(1)}, u32[]{:S(2)}, u32[]{:S(2)}) collective-permute-start(f32[1536,128]{1,0:T(8,128)S(1)} %bitcast.25), channel_id=1, source_target_pairs={{0,1},{1,0},{2,3},{3,2},{4,5},{5,4},{6,7},{7,6},{8,9},{9,8},{10,11... | collective-permute-start | bytes 2359304 | tf_op jit(solution)/shard_map/ppermute | solution.py:477
  27.6 1.7 %receivers.1.wtab = bf16[192,64,384]{2,1,0:T(8,128)(2,1)S(1)} custom-call(f32[288,128]{1,0:T(8,128)S(1)} %join.1.refs_0_, f32[288,128]{1,0:T(8,128)S(1)} %collective-permute-done.2.refs_1_, f32[288,128]{1,0:T(8,128)S(1)} %collective-permute-done.3.refs_2_, f32[288,128]{1,0:T(8,128)S(1)} %collective-permute-done.4.refs_3_), custom_call_target="tpu_custom_call" | custom-call | flops 4400000000 | bytes 65536 | tf_op jit(solution)/shard_map/receivers/pallas_call | solution.py:478
  29.2 0.0 collective-permute-done.5.far
  29.2 0.0 copy-done
  29.3 0.0 copy-done.8
  29.3 0.0 copy-done.9
  29.3 0.0 copy-start.1
  29.3 0.0 copy-start.4
  29.3 0.0 copy-start.5
  29.3 0.0 copy-start.6
  29.3 0.0 copy-start.7
  29.3 0.0 copy-start.10
  29.3 0.0 copy-start.11
  29.4 0.0 copy-start.12
  29.4 9.8 %pairs.1 = f32[384,128]{1,0:T(8,128)S(1)} custom-call(s32[1]{0:T(128)} %bitcast.24.count, s32[512]{0:T(512)S(1)} %bitcast.37, s32[512]{0:T(512)S(1)} %bitcast.38, s32[3]{0:T(128)S(1)} %copy-done, f32[1536,128]{1,0:T(8,128)S(1)} %bitcast.26, f32[1536,128]{1,0:T(8,128)S(1)} %collective-permute-done.5.far, bf16[192,64,384]{2,1,0:T(8,128)(2,1)S(1)} %receivers.1.wtab), custom_call_target="tpu_custom_call" | custom-call | flops 22000001024 | bytes 65536 | tf_op jit(solution)/shard_map/pairs/pallas_call | solution.py:487
  39.2 13.9 %all_to_all.27 = f32[8,1,6144]{2,1,0:T(1,128)S(1)} all-to-all(f32[8,1,6144]{2,1,0:T(1,128)S(1)} %bitcast.27), channel_id=1, replica_groups=mesh['pair'=2,'ring'=4,'half'=8,'core'=2] {'pair','ring'}, dimensions={0} | all-to-all | bytes 393216 | tf_op jit(solution)/shard_map/all_to_all | solution.py:508
  53.1 0.0 copy-done.1
  53.1 0.0 copy-done.4
  53.1 0.0 copy-done.5
  53.1 0.0 copy-done.6
  53.1 0.0 copy-done.7
  53.1 0.0 copy-done.10
  53.1 0.0 copy-done.11
  53.2 0.0 copy-done.12
  53.2 0.8 %loads.1 = (f32[256,128]{1,0:T(8,128)S(1)}, f32[24,128]{1,0:T(8,128)S(1)}) custom-call(f32[384,128]{1,0:T(8,128)S(1)} %bitcast.28, f32[8,3072]{1,0:T(8,128)S(1)} %copy-done.1, f32[24,128]{1,0:T(8,128)S(1)} %bitcast.35, f32[24,128]{1,0:T(8,128)S(1)} %bitcast.36, f32[24,128]{1,0:T(8,128)S(1)} %bitcast.34, s32[24,128]{1,0:T(8,128)S(1)} %bitcast.32, ...), custom_call_target="tpu_custom_call" | custom-call | flops 1100000000 | bytes 65536 | tf_op jit(solution)/shard_map/loads/pallas_call | solution.py:509
  54.0 18.9 %all_to_all.28 = f32[128,1,256]{2,1,0:T(1,128)S(1)} all-to-all(f32[128,1,256]{2,1,0:T(1,128)S(1)} %bitcast.29), channel_id=1, replica_groups=mesh['pair'=2,'ring'=4,'half'=8,'core'=2] {'pair','ring','half','core'}, dimensions={0} | all-to-all | bytes 262144 | tf_op jit(solution)/shard_map/all_to_all | solution.py:525
  72.9 1.9 %finish.1 = (f32[24,128]{1,0:T(8,128)}, f32[1,9]{1,0:T(1,128)}, f32[16,128]{1,0:T(8,128)}) custom-call(f32[256,128]{1,0:T(8,128)S(1)} %bitcast.30, f32[8,3072]{1,0:T(8,128)S(1)} %copy-done.1, f32[24,128]{1,0:T(8,128)S(1)} %get-tuple-element.37.damped), custom_call_target="tpu_custom_call" | custom-call | flops 1100000000 | bytes 65536 | tf_op jit(solution)/shard_map/finish/pallas_call | solution.py:526
Async XLA Ops:
  0.6 12.6 %copy-start.2 = (f32[3,3072]{1,0:T(4,128)S(1)}, f32[3,3072]{1,0:T(4,128)}, u32[]{:S(2)}) copy-start(f32[3,3072]{1,0:T(4,128)} %own_pos.1) | copy-start | bytes 110596
  0.6 12.5 %copy-start.3 = (f32[3,3072]{1,0:T(4,128)S(1)}, f32[3,3072]{1,0:T(4,128)}, u32[]{:S(2)}) copy-start(f32[3,3072]{1,0:T(4,128)} %own_nor.1) | copy-start | bytes 110596
  0.7 12.5 %collective-permute-start = (f32[3,3072]{1,0:T(4,128)}, f32[3,3072]{1,0:T(4,128)S(1)}, u32[]{:S(2)}, u32[]{:S(2)}) collective-permute-start(f32[3,3072]{1,0:T(4,128)} %own_pos.1), channel_id=1, source_target_pairs={{0,64},{64,0},{1,65},{65,1},{2,66},{66,2},{3,67},{67,3},{4,68},{68... | collective-permute-start | bytes 110600 | tf_op jit(solution)/shard_map/ppermute | solution.py:429
  2.8 10.4 %collective-permute-start.1 = (f32[3,3072]{1,0:T(4,128)}, f32[3,3072]{1,0:T(4,128)S(1)}, u32[]{:S(2)}, u32[]{:S(2)}) collective-permute-start(f32[3,3072]{1,0:T(4,128)} %own_nor.1), channel_id=1, source_target_pairs={{0,64},{64,0},{1,65},{65,1},{2,66},{66,2},{3,67},{67,3},{4,68},{68... | collective-permute-start | bytes 110600 | tf_op jit(solution)/shard_map/ppermute | solution.py:429
  4.8 18.5 %all-to-all-start = ((f32[8,1,24576]{2,1,0:T(1,128)}), f32[8,1,24576]{2,1,0:T(1,128)S(1)}, u32[]{:S(2)}, u32[]{:S(2)}) async-start(f32[8,1,24576]{2,1,0:T(1,128)} %bitcast.39), calls=%async_computation | async-start | bytes 1572864 | tf_op jit(solution)/shard_map/all_to_all | solution.py:473
  13.3 8.0 %collective-permute-start.2 = (f32[288,128]{1,0:T(8,128)S(1)}, f32[288,128]{1,0:T(8,128)S(1)}, u32[]{:S(2)}, u32[]{:S(2)}) collective-permute-start(f32[288,128]{1,0:T(8,128)S(1)} %join.1.refs_0_), channel_id=1, source_target_pairs={{0,16},{16,32},{32,48},{48,0},{1,17},{17,33},{33,49},{49,1},{2,18}... | collective-permute-start | bytes 442376 | tf_op jit(solution)/shard_map/ppermute | solution.py:470
  14.7 7.8 %collective-permute-start.3 = (f32[288,128]{1,0:T(8,128)S(1)}, f32[288,128]{1,0:T(8,128)S(1)}, u32[]{:S(2)}, u32[]{:S(2)}) collective-permute-start(f32[288,128]{1,0:T(8,128)S(1)} %join.1.refs_0_), channel_id=1, source_target_pairs={{0,32},{16,48},{32,0},{48,16},{1,33},{17,49},{33,1},{49,17},{2,34}... | collective-permute-start | bytes 442376 | tf_op jit(solution)/shard_map/ppermute | solution.py:470
  17.3 5.7 %collective-permute-start.4 = (f32[288,128]{1,0:T(8,128)S(1)}, f32[288,128]{1,0:T(8,128)S(1)}, u32[]{:S(2)}, u32[]{:S(2)}) collective-permute-start(f32[288,128]{1,0:T(8,128)S(1)} %join.1.refs_0_), channel_id=1, source_target_pairs={{0,48},{16,0},{32,16},{48,32},{1,49},{17,1},{33,17},{49,33},{2,50}... | collective-permute-start | bytes 442376 | tf_op jit(solution)/shard_map/ppermute | solution.py:470
  21.3 8.0 %copy-start = (s32[3]{0:T(128)S(1)}, s32[3]{0:T(128)}, u32[]{:S(2)}) copy-start(s32[3]{0:T(128)} %pad_add_fusion.place) | copy-start | bytes 40
  21.3 8.0 %copy-start.8 = (s32[4,128]{1,0:T(4,128)S(1)}, s32[4,128]{1,0:T(4,128)}, u32[]{:S(2)}) copy-start(s32[4,128]{1,0:T(4,128)} %get-tuple-element.26) | copy-start | bytes 6148
  21.3 8.0 %copy-start.9 = (s32[4,128]{1,0:T(4,128)S(1)}, s32[4,128]{1,0:T(4,128)}, u32[]{:S(2)}) copy-start(s32[4,128]{1,0:T(4,128)} %get-tuple-element.27) | copy-start | bytes 6148
  23.3 5.9 %collective-permute-start.5 = (f32[1536,128]{1,0:T(8,128)S(1)}, f32[1536,128]{1,0:T(8,128)S(1)}, u32[]{:S(2)}, u32[]{:S(2)}) collective-permute-start(f32[1536,128]{1,0:T(8,128)S(1)} %bitcast.25), channel_id=1, source_target_pairs={{0,1},{1,0},{2,3},{3,2},{4,5},{5,4},{6,7},{7,6},{8,9},{9,8},{10,11... | collective-permute-start | bytes 2359304 | tf_op jit(solution)/shard_map/ppermute | solution.py:477
  29.3 23.8 %copy-start.1 = (f32[8,3072]{1,0:T(8,128)S(1)}, f32[8,3072]{1,0:T(8,128)}, u32[]{:S(2)}) copy-start(f32[8,3072]{1,0:T(8,128)} %basis.7) | copy-start | bytes 294916
  29.3 23.8 %copy-start.4 = (s32[3072,1]{0,1:T(1,128)S(1)}, s32[3072,1]{0,1:T(1,128)}, u32[]{:S(2)}) copy-start(s32[3072,1]{0,1:T(1,128)} %param.22) | copy-start | bytes 36868
  29.3 23.8 %copy-start.5 = (f32[3072]{0:T(1024)S(1)}, f32[3072]{0:T(1024)}, u32[]{:S(2)}) copy-start(f32[3072]{0:T(1024)} %param.14) | copy-start | bytes 36868
  29.3 23.8 %copy-start.6 = (f32[3072]{0:T(1024)S(1)}, f32[3072]{0:T(1024)}, u32[]{:S(2)}) copy-start(f32[3072]{0:T(1024)} %param.15) | copy-start | bytes 36868
  29.3 23.8 %copy-start.7 = (f32[3072]{0:T(1024)S(1)}, f32[3072]{0:T(1024)}, u32[]{:S(2)}) copy-start(f32[3072]{0:T(1024)} %param.16) | copy-start | bytes 36868
  29.3 23.8 %copy-start.10 = (f32[128,128]{1,0:T(8,128)S(1)}, f32[128,128]{1,0:T(8,128)}, u32[]{:S(2)}) copy-start(f32[128,128]{1,0:T(8,128)} %get-tuple-element.34.slots) | copy-start | bytes 196612
  29.3 23.8 %copy-start.11 = (s32[24,128]{1,0:T(8,128)S(1)}, s32[24,128]{1,0:T(8,128)}, u32[]{:S(2)}) copy-start(s32[24,128]{1,0:T(8,128)} %get-tuple-element.33.rank) | copy-start | bytes 36868
  29.4 23.8 %copy-start.12 = (f32[1,128]{1,0:T(1,128)S(1)}, f32[1,128]{1,0:T(1,128)}, u32[]{:S(2)}) copy-start(f32[1,128]{1,0:T(1,128)} %get-tuple-element.35.gram) | copy-start | bytes 1540
